TPU v7x, 32 devices: a whole 2x2x4 slice. The times are simulated.
32 devices in a mesh: groups: 2 (over x), tm: 16 (over z, y, core).
Axes of the slice: x: 2, y: 2, z: 4, core: 2. Of those that a mesh axis runs over, the one named last changes fastest.
Arguments:
- latent: bfloat16 [16384, 384], P(('groups', 'tm')), parts along dimension 0, may hold values from -45 to 45
- owner: int32 [16384], P(('groups', 'tm')), parts along dimension 0, may hold values from 0 to 15, as said below
- frame_counts: int32 [16], P('groups'), parts along dimension 0, may hold values from 1 to 8, 32 in all
- norm_gain: float32 [384], replicated, may hold values from 0.1 to 1.9
- norm_shift: float32 [384], replicated, may hold values from -3 to 3
- res_kernel: bfloat16 [3, 3, 3, 384, 384], replicated, may hold values from -0.0625 to 0.0625
- res_bias: float32 [384], replicated, may hold values from -3 to 3
- time_kernel: bfloat16 [3, 384, 768], replicated, may hold values from -0.1875 to 0.1875
- time_bias: float32 [768], replicated, may hold values from -3 to 3
- up_kernel: bfloat16 [3, 3, 384, 192], replicated, may hold values from -0.109375 to 0.109375
- up_bias: float32 [192], replicated, may hold values from -3 to 3
Outputs:
- frames_out: bfloat16 [128, 32, 6144], P(('groups', 'tm')), parts along dimension 0
There are 2 independent parts, one for each index of `groups`. A program takes and returns all parts, laid end to end along the dimension named above; an argument that names none is the same for every part. Nothing has to cross between parts.
Inputs may be any that keep to these rules, and one draw needn't show every extreme that they name: Each device's block of 512 tokens holds at most 64 tokens for any one owner, some block holds exactly 64 for one owner, and every device is the owner of exactly 512 tokens.
All inputs are finite; a program needn't handle non-finite values.
Results may differ from a plain program's by a relative error of at most 0.0057.
Values may be sent and summed in bfloat16 or wider, within the bound.
No kernel may reach another device: no remote copies, remote signals or barrier semaphores. Data moves between devices by JAX's collectives and lax.ppermute only.
A program may use at most 128 MiB of HBM per device.

v0:
```python
import functools

import jax
import jax.numpy as jnp
from jax import lax
from jax.experimental import pallas as pl
from jax.experimental.pallas import tpu as pltpu
from jax.sharding import PartitionSpec as P

H = 16
W = 16
MARK = 128.0
epsilon = 1e-06
MIB = 1 << 20
f32 = jnp.float32
bf16 = jnp.bfloat16


def in_vmem(value):
    return pltpu.with_memory_space_constraint(value, pltpu.VMEM)


def in_hbm(value):
    return pltpu.with_memory_space_constraint(value, pltpu.HBM)


VM = pl.BlockSpec(memory_space=pltpu.VMEM)
HB = pl.BlockSpec(memory_space=pltpu.HBM)
SM = pl.BlockSpec(memory_space=pltpu.SMEM)


def iota(shape, dim):
    return lax.broadcasted_iota(jnp.int32, shape, dim)


def mm(lhs, rhs):
    return jnp.dot(lhs, rhs, preferred_element_type=f32)


def convolve(near, taps):
    return lax.dot_general(taps, near, (((0,), (1,)), ((), ())), preferred_element_type=f32).T


def from_behind(value, axis):
    size = lax.axis_size(axis)
    return lax.ppermute(value, axis, [(i, (i + 1) % size) for i in range(size)])


def pack_kernel(
    owner_hbm, latent_hbm, out_hbm, owner_ref, wide_ref, made_ref, arrived, left, *, peers, capacity
):
    tokens, channels = latent_hbm.shape
    copies = [
        pltpu.make_async_copy(owner_hbm, owner_ref, arrived.at[0]),
        pltpu.make_async_copy(latent_hbm, wide_ref.at[:, :channels], arrived.at[1]),
    ]
    for copy in copies:
        copy.start()
    wide_ref[:, channels:] = jnp.ones((tokens, 128), bf16)
    upper = (iota((tokens, tokens), 0) <= iota((tokens, tokens), 1)).astype(bf16)
    copies[0].wait()
    owner = owner_ref[...]
    marked = iota((peers, tokens), 0) == owner
    running = mm(marked.astype(bf16), upper)
    rank = jnp.sum(jnp.where(marked, running - 1.0, 0.0), 0, keepdims=True)
    slot = owner * capacity + rank.astype(jnp.int32)
    copies[1].wait()
    pieces = left.shape[0]
    rows = peers * capacity // pieces
    sent = []
    for piece in range(pieces):
        at = pl.ds(piece * rows, rows)
        chosen = (iota((rows, tokens), 0) + piece * rows == slot).astype(bf16)
        found = mm(chosen, wide_ref[...])
        empty = (1.0 - found[:, channels:]) * MARK
        made_ref[at] = (
            found[:, :channels] + jnp.concatenate([empty] * (channels // 128), 1)
        ).astype(bf16)
        copy = pltpu.make_async_copy(made_ref.at[at], out_hbm.at[at], left.at[piece])
        copy.start()
        sent.append(copy)
    for copy in sent:
        copy.wait()


def places(got_ref, peers, capacity):
    slots = got_ref.shape[0]
    present = (got_ref[:, :128] < MARK / 2).astype(bf16)
    sender = iota((peers, slots), 1) // capacity
    member = (sender == iota((peers, slots), 0)).astype(f32)
    below = (sender < iota((peers, slots), 0)).astype(f32)
    tallies = mm(jnp.concatenate([member, below], 0).astype(bf16), present)
    held = jnp.sum(member * tallies[:peers, :1], 0, keepdims=True).astype(jnp.int32)
    first = jnp.sum(member * tallies[peers:, :1], 0, keepdims=True).astype(jnp.int32)
    within = iota((1, slots), 1) % capacity
    return jnp.where(within < held, first + within, -1)


def unpack(place, got_ref, small_ref, decoded_ref, active_ref, frame):
    slots, channels = got_ref.shape
    pixels = decoded_ref.shape[0]
    pixel = iota((pixels, slots), 0)
    source = frame * pixels + (pixel % H) * W + pixel // H
    chosen = (source == place).astype(bf16)
    values = mm(chosen, got_ref[...])
    decoded_ref[...] = values.astype(bf16)
    squares = jnp.mean(values * values, -1, keepdims=True)
    scaled = values * lax.rsqrt(squares + epsilon)
    fed = scaled * small_ref[0:1, :channels] + small_ref[1:2, :channels]
    active_ref[...] = (fed / (1.0 + jnp.exp(-fed))).astype(bf16)


def unpack_second_kernel(
    got_ref, small_ref, decoded_ref, active_ref, place_ref, *, peers, capacity
):
    place = places(got_ref, peers, capacity)
    place_ref[...] = place
    unpack(place, got_ref, small_ref, decoded_ref, active_ref, 1)


def unpack_first_kernel(got_ref, small_ref, place_ref, decoded_ref, active_ref):
    unpack(place_ref[...], got_ref, small_ref, decoded_ref, active_ref, 0)


def vertical(frame):
    wide = frame.astype(f32)
    y = iota(wide.shape, 0) % H
    up = jnp.where(y == 0, 0.0, pltpu.roll(wide, 1, 0))
    down = jnp.where(y == H - 1, 0.0, pltpu.roll(wide, wide.shape[0] - 1, 0))
    return up.astype(bf16), frame, down.astype(bf16)


def steps(frame):
    wide = frame.astype(f32)
    up, here, down = vertical(frame)
    return (up.astype(f32) - wide).astype(bf16), here, (down.astype(f32) - wide).astype(bf16)


def patches(frame):
    pixels, channels = frame.shape
    nothing = jnp.zeros((H, channels), bf16)
    parts = []
    for shifted in vertical(frame):
        parts.append(jnp.concatenate([nothing, shifted[: pixels - H]], 0))
        parts.append(shifted)
        parts.append(jnp.concatenate([shifted[H:], nothing], 0))
    return jnp.concatenate(parts, 1)


def kept(keep_ref):
    return [[keep_ref[3 * f + back : 3 * f + back + 1, :1] for back in range(3)] for f in range(2)]


def local_conv_kernel(
    keep_ref, first_ref, second_ref, here_ref, behind_ref, sum0_ref, sum1_ref
):
    keep = kept(keep_ref)
    channels = sum0_ref.shape[1]
    sum1 = convolve(patches(second_ref[...]), here_ref[...])
    both = mm(
        patches(first_ref[...]), jnp.concatenate([here_ref[...], behind_ref[...]], 1)
    )
    sum0_ref[...] = both[:, :channels]
    sum1_ref[...] = sum1 + keep[1][1] * both[:, channels:]


def second_residual_kernel(
    solo_ref, keep_ref, small_ref, prior_ref, far_ref, sum_ref, decoded_ref, out_ref, near_ref
):
    base = sum_ref[...] + decoded_ref[...].astype(f32) + small_ref[2:3, : out_ref.shape[1]]


    @pl.when(solo_ref[0] == 1)
    def _():
        out_ref[...] = base.astype(bf16)

    @pl.when(solo_ref[0] == 0)
    def _():
        near = patches(prior_ref[...])
        near_ref[...] = near
        far = kept(keep_ref)[1][2] * convolve(near, far_ref[...])
        out_ref[...] = (base + far).astype(bf16)


def behind_kernel(
    solo_ref, keep_ref, small_ref, near_ref, behind_ref, sum_ref, decoded_ref, out_ref
):
    base = sum_ref[...] + decoded_ref[...].astype(f32) + small_ref[2:3, : out_ref.shape[1]]

    @pl.when(solo_ref[0] == 1)
    def _():
        out_ref[...] = base

    @pl.when(solo_ref[0] == 0)
    def _():
        out_ref[...] = base + kept(keep_ref)[0][1] * convolve(near_ref[...], behind_ref[...])


def first_residual_kernel(solo_ref, keep_ref, prior_ref, far_ref, sum_ref, out_ref):

    @pl.when(solo_ref[0] == 1)
    def _():
        out_ref[...] = sum_ref[...].astype(bf16)

    @pl.when(solo_ref[0] == 0)
    def _():
        far = kept(keep_ref)[0][2] * convolve(patches(prior_ref[...]), far_ref[...])
        out_ref[...] = (sum_ref[...] + far).astype(bf16)


def local_time_kernel(
    keep_ref, small_ref, first_ref, second_ref, time_ref, sum0_ref, sum1_ref
):
    keep = kept(keep_ref)
    bias = small_ref[3:4, : sum0_ref.shape[1]]
    sum0_ref[...] = mm(first_ref[...], time_ref[2]) + bias
    sum1_ref[...] = (
        mm(second_ref[...], time_ref[2]) + bias + keep[1][1] * mm(first_ref[...], time_ref[1])
    )


def upscale(temporal, frame, small_ref, folded_ref, made_ref, near, rows32, ready=()):
    pixels = H * W
    channels = near.shape[1] // 3
    outs = folded_ref.shape[3]
    both = temporal.astype(bf16)
    nothing = jnp.zeros((H, 3 * channels), bf16)
    for half in range(2):
        base = H + half * (pixels + H)
        near[base - H : base] = nothing
        shown = both[:, half * channels : (half + 1) * channels]
        for t, part in enumerate(steps(shown)):
            near[base : base + pixels, t * channels : (t + 1) * channels] = part
    near[2 * (H + pixels) :] = nothing
    span = 2 * pixels + H
    bias = small_ref[4:5, :outs]
    blocks = 2 * outs // 128
    products = []
    for q in range(2):
        for t in range(3):
            windows = [
                near[(q + side) * H : (q + side) * H + span, t * channels : (t + 1) * channels]
                for side in range(2)
            ]
            products.append(mm(jnp.concatenate(windows, 1), folded_ref[q, t]))
    for p in range(2):
        pair = jnp.concatenate(
            [products[3 * q + 1] + bias + products[3 * q + 2 * p] for q in range(2)], 1
        )
        for half in range(2):
            for x in range(W):
                row = half * (pixels + H) + x * H
                for block in range(blocks):
                    rows32[half, x * blocks + block, pl.ds(p, H, stride=2)] = pair[
                        row : row + H, block * 128 : (block + 1) * 128
                    ]
    for half in range(2):
        for block in range(W * blocks):
            made_ref[2 * frame + half, :, block * 128 : (block + 1) * 128] = rows32[
                half, block
            ].astype(bf16)
        for copy in ready[half : half + 1]:
            copy.start()


def early_up_kernel(
    solo_ref, small_ref, sum0_ref, sum1_ref, folded_ref, out_hbm, made_ref, near, rows32, left
):
    @pl.when(solo_ref[0] == 1)
    def _():
        copies = [
            pltpu.make_async_copy(made_ref.at[e], out_hbm.at[e], left.at[e]) for e in range(4)
        ]
        for f, sum_ref in ((1, sum1_ref), (0, sum0_ref)):
            ready = copies[2 * f : 2 * f + 2]
            upscale(sum_ref[...], f, small_ref, folded_ref, made_ref, near, rows32, ready)
        for copy in copies:
            copy.wait()


def second_up_kernel(
    solo_ref, keep_ref, small_ref, prior_ref, time_ref, sum_ref, folded_ref, made_ref, near, rows32
):
    @pl.when(solo_ref[0] == 0)
    def _():
        temporal = sum_ref[...] + kept(keep_ref)[1][2] * mm(prior_ref[...], time_ref[0])
        upscale(temporal, 0, small_ref, folded_ref, made_ref, near, rows32)


def first_up_kernel(
    solo_ref, keep_ref, small_ref, before_ref, prior_ref, time_ref, sum_ref, folded_ref,
    later_ref, early_hbm, out_hbm,
    made_ref, near, rows32, left,
):
    @pl.when(solo_ref[0] == 0)
    def _():
        later = pltpu.make_async_copy(later_ref, out_hbm.at[2:4], left.at[0])
        later.start()
        seen = [keep_ref[row : row + 1, :1].astype(bf16) for row in (2, 1)]
        pair = jnp.concatenate([before_ref[...] * seen[0], prior_ref[...] * seen[1]], 1)
        both = time_ref[:2].reshape(pair.shape[1], time_ref.shape[2])
        temporal = sum_ref[...] + mm(pair, both)
        copies = [
            pltpu.make_async_copy(made_ref.at[e], out_hbm.at[e], left.at[1 + e]) for e in range(2)
        ]
        upscale(temporal, 0, small_ref, folded_ref, made_ref, near, rows32, copies)
        for copy in copies:
            copy.wait()
        later.wait()


def keeps(counts_ref, position_ref):
    first = position_ref[0] * 2
    starts = [jnp.int32(0), jnp.int32(0)]
    end = jnp.int32(0)
    for video in range(counts_ref.shape[0]):
        end = end + counts_ref[video]
        starts = [jnp.where(end <= first + f, end, starts[f]) for f in range(2)]
    return [
        [(first + f - back >= starts[f]).astype(f32) for back in range(3)] for f in range(2)
    ]


def halves(taps):
    return (taps[0], taps[1] + taps[2]), (taps[0] + taps[1], taps[2])


def prepare_kernel(
    counts_ref, position_ref, gain_ref, shift_ref, res_bias_ref, time_bias_ref, up_bias_ref,
    up_hbm, taps_hbm,
    folded_hbm, small_ref, keep_ref, here_ref, behind_hbm, far_hbm, solo_ref,
    up_ref, folded_ref, behind_ref, far_ref, arrived, left,
):
    copies = [
        pltpu.make_async_copy(up_hbm, up_ref, arrived.at[0]),
        pltpu.make_async_copy(taps_hbm.at[2], here_ref, arrived.at[1]),
        pltpu.make_async_copy(taps_hbm.at[1], behind_ref, arrived.at[2]),
        pltpu.make_async_copy(taps_hbm.at[0], far_ref, arrived.at[3]),
    ]
    for copy in copies:
        copy.start()
    small_ref[...] = jnp.zeros_like(small_ref)
    for i, ref in enumerate((gain_ref, shift_ref, res_bias_ref, time_bias_ref, up_bias_ref)):
        small_ref[i : i + 1, : ref.shape[1]] = ref[...]
    keep = keeps(counts_ref, position_ref)
    solo_ref[0] = (keep[0][1] == 0.0).astype(jnp.int32)
    row = iota(keep_ref.shape, 0)
    seen = jnp.zeros(keep_ref.shape, f32)
    for f in range(2):
        for back in range(3):
            seen = jnp.where(row == 3 * f + back, keep[f][back], seen)
    keep_ref[...] = seen
    copies[0].wait()
    channels = up_ref.shape[3]
    rows = [[up_ref[a, b].astype(f32) for b in range(3)] for a in range(3)]
    rows[1] = [rows[0][b] + rows[1][b] + rows[2][b] for b in range(3)]
    for t in range(3):
        columns = halves(rows[t])
        for q in range(2):
            for side in range(2):
                folded_ref[q, t, side * channels : (side + 1) * channels] = columns[q][
                    side
                ].T.astype(bf16)
    for copy in copies[1:]:
        copy.wait()
    sent = [
        pltpu.make_async_copy(behind_ref, behind_hbm, left.at[0]),
        pltpu.make_async_copy(far_ref, far_hbm, left.at[1]),
        pltpu.make_async_copy(folded_ref, folded_hbm, left.at[2]),
    ]
    for copy in sent:
        copy.start()
    for copy in sent:
        copy.wait()


def on_device(
    latent,
    owner,
    frame_counts,
    norm_gain,
    norm_shift,
    res_kernel,
    res_bias,
    time_kernel,
    time_bias,
    up_kernel,
    up_bias,
):
    peers = lax.axis_size("tm")
    position = lax.axis_index("tm").astype(jnp.int32).reshape(1)
    tokens, channels = latent.shape
    capacity = 2 * tokens // peers
    pixels = H * W
    wide = time_kernel.shape[-1]
    outs = up_kernel.shape[-1]

    packed = pl.pallas_call(
        functools.partial(pack_kernel, peers=peers, capacity=capacity),
        out_shape=jax.ShapeDtypeStruct((peers * capacity, channels), bf16),
        in_specs=[HB, HB],
        out_specs=HB,
        scratch_shapes=[
            pltpu.VMEM((1, tokens), jnp.int32),
            pltpu.VMEM((tokens, channels + 128), bf16),
            pltpu.VMEM((peers * capacity, channels), bf16),
            pltpu.SemaphoreType.DMA((2,)),
            pltpu.SemaphoreType.DMA((4,)),
        ],
        compiler_params=pltpu.CompilerParams(vmem_limit_bytes=16 * MIB),
        name="pack",
    )(in_hbm(owner.reshape(1, tokens)), in_hbm(latent))
    packed, up_kernel = lax.optimization_barrier((packed, up_kernel))
    received = lax.all_to_all(packed, "tm", split_axis=0, concat_axis=0, tiled=True)
    res_kernel = res_kernel.reshape(3, 9 * channels, channels)
    one_tap = (9 * channels, channels)
    res_kernel = in_hbm(res_kernel)
    folded, small, keep, here, behind, far, solo = pl.pallas_call(
        prepare_kernel,
        out_shape=[
            pltpu.HBM((2, 3, 2 * channels, outs), bf16),
            pltpu.VMEM((8, wide), f32),
            pltpu.VMEM((8, 128), f32),
            pltpu.VMEM(one_tap, bf16),
            pltpu.HBM(one_tap, bf16),
            pltpu.HBM(one_tap, bf16),
            pltpu.SMEM((1,), jnp.int32),
        ],
        in_specs=[SM] * 2 + [VM] * 5 + [HB] * 2,
        out_specs=[HB] + [VM] * 3 + [HB] * 2 + [SM],
        scratch_shapes=[
            pltpu.VMEM((3, 3, outs, channels), bf16),
            pltpu.VMEM((2, 3, 2 * channels, outs), bf16),
            pltpu.VMEM(one_tap, bf16),
            pltpu.VMEM(one_tap, bf16),
            pltpu.SemaphoreType.DMA((4,)),
            pltpu.SemaphoreType.DMA((3,)),
        ],
        compiler_params=pltpu.CompilerParams(vmem_limit_bytes=20 * MIB),
        cost_estimate=pl.CostEstimate(
            flops=0, bytes_accessed=2 * res_kernel.size * 2, transcendentals=0
        ),
        name="prepare",
    )(
        frame_counts,
        position,
        norm_gain.reshape(1, channels),
        norm_shift.reshape(1, channels),
        res_bias.reshape(1, channels),
        time_bias.reshape(1, wide),
        up_bias.reshape(1, outs),
        in_hbm(jnp.swapaxes(up_kernel, 2, 3)),
        res_kernel,
    )

    def call(body, name, outputs, arguments, scratch=(), share=1.0, **more):
        out_specs = more.pop("out_specs", [VM] * len(outputs))
        in_specs = more.pop("in_specs", [VM] * len(arguments))
        return pl.pallas_call(
            body,
            out_shape=outputs,
            in_specs=in_specs,
            out_specs=out_specs,
            scratch_shapes=scratch,
            compiler_params=pltpu.CompilerParams(vmem_limit_bytes=12 * MIB),
            cost_estimate=pl.CostEstimate(
                flops=int(share * tap), bytes_accessed=0, transcendentals=0
            ),
            name=name,
            **more,
        )(*arguments)

    vm = in_vmem
    frame16 = pltpu.VMEM((pixels, channels), bf16)
    frame32 = pltpu.VMEM((pixels, channels), f32)
    near_shape = pltpu.VMEM((pixels, 9 * channels), bf16)
    tap = 2 * pixels * 9 * channels * channels
    sem = pltpu.SemaphoreType.DMA
    small, keep, received = vm(small), vm(keep), vm(received)
    decoded1, active1, place = call(
        functools.partial(unpack_second_kernel, peers=peers, capacity=capacity),
        "unpack_second",
        [frame16] * 2 + [pltpu.VMEM((1, peers * capacity), jnp.int32)],
        [received, small],
        share=3,
    )
    prior1 = from_behind(active1, "tm")
    decoded0, active0 = call(
        unpack_first_kernel, "unpack_first", [frame16] * 2, [received, small, vm(place)], share=0
    )
    prior0 = from_behind(active0, "tm")
    behind, far = vm(behind), vm(far)
    sum0, sum1 = call(
        local_conv_kernel,
        "local_conv",
        [frame32] * 2,
        [keep, vm(active0), vm(active1), vm(here), behind],
        share=3,
    )
    second, near = call(
        second_residual_kernel,
        "second_residual",
        [frame16, near_shape],
        [solo, keep, small, vm(prior1), far, vm(sum1), vm(decoded1)],
        in_specs=[SM] + [VM] * 6,
        share=1,
    )
    prior_second = from_behind(second, "tm")
    (sum0,) = call(
        behind_kernel,
        "behind",
        [frame32],
        [solo, keep, small, vm(near), behind, vm(sum0), vm(decoded0)],
        in_specs=[SM] + [VM] * 6,
        share=1,
    )
    (first,) = call(
        first_residual_kernel,
        "first_residual",
        [frame16],
        [solo, keep, vm(prior0), far, vm(sum0)],
        in_specs=[SM] + [VM] * 4,
        share=1,
    )
    prior_first = from_behind(first, "tm")
    times = vm(time_kernel)
    time0, time1 = call(
        local_time_kernel,
        "local_time",
        [pltpu.VMEM((pixels, wide), f32)] * 2,
        [keep, small, vm(first), vm(second), times],
        share=0.4,
    )
    frames = 2 * tokens // pixels
    shape = (frames, 2 * H, 2 * W * outs)
    up_scratch = [
        pltpu.VMEM((2 * pixels + 3 * H, 3 * channels), bf16),
        pltpu.VMEM((2, 2 * W * outs // 128, 2 * H, 128), f32),
    ]
    folded, prior_second = vm(folded), vm(prior_second)
    time0, time1 = vm(time0), vm(time1)
    half_shape = (frames // 2,) + shape[1:]
    (early,) = call(
        early_up_kernel,
        "early_up",
        [jax.ShapeDtypeStruct(shape, bf16)],
        [solo, small, time0, time1, folded],
        [pltpu.VMEM(shape, bf16)] + up_scratch + [sem((4,))],
        share=2,
        in_specs=[SM] + [VM] * 4,
        out_specs=[HB],
    )
    (later,) = call(
        second_up_kernel,
        "second_up",
        [pltpu.VMEM(half_shape, bf16)],
        [solo, keep, small, prior_second, times, time1, folded],
        up_scratch,
        share=6,
        in_specs=[SM] + [VM] * 6,
    )
    (made,) = call(
        first_up_kernel,
        "first_up",
        [jax.ShapeDtypeStruct(shape, bf16)],
        [
            solo, keep, small, vm(prior_first), prior_second, times, time0, folded, vm(later),
            early,
        ],
        [pltpu.VMEM(half_shape, bf16)] + up_scratch + [sem((3,))],
        share=6,
        in_specs=[SM] + [VM] * 8 + [pl.BlockSpec(memory_space=pl.ANY)],
        out_specs=[HB],
        input_output_aliases={9: 0},
    )
    return made


def solution(mesh):
    placed = (
        P(("groups", "tm"), None),
        P(("groups", "tm")),
        P("groups"),
        P(),
        P(),
        P(),
        P(),
        P(),
        P(),
        P(),
        P(),
    )
    return jax.shard_map(
        on_device,
        mesh=mesh,
        in_specs=placed,
        out_specs=P(("groups", "tm"), None, None),
        check_vma=False,
    )
```

profile of v0, /device:TPU:0, one launch (start us, length us, event | category | flops | bytes accessed | tf_op | source)
XLA Modules:
  0.0 47.8 jit_solution(15892021249873063097)
XLA Ops:
  0.0 0.0 copy-start.5
  0.0 2.5 %pack.1 = bf16[1024,384]{1,0:T(8,128)(2,1)} custom-call(s32[1,512]{1,0:T(1,128)} %bitcast.12, bf16[512,384]{1,0:T(8,128)(2,1)} %latent_hbm.1), custom_call_target="tpu_custom_call" | custom-call | tf_op jit(solution)/shard_map/pack/pallas_call | solution.py:398
  2.6 7.4 %all-to-all-start = ((bf16[16,64,384]{2,1,0:T(8,128)(2,1)}), bf16[16,64,384]{2,1,0:T(8,128)(2,1)S(1)}, u32[]{:S(2)}, u32[]{:S(2)}) async-start(bf16[16,64,384]{2,1,0:T(8,128)(2,1)} %bitcast.5), calls=%async_computation | async-start | bytes 1572864 | tf_op jit(solution)/shard_map/all_to_all | solution.py:414
  10.0 0.0 copy-done.7
  10.0 0.0 copy-done.8
  10.0 0.0 copy-done.9
  10.0 0.0 copy-done.6
  10.1 0.0 copy-done.4
  10.1 0.0 copy-done.5
  10.1 7.3 %prepare.1 = (bf16[2,3,768,192]{3,2,1,0:T(8,128)(2,1)}, f32[8,768]{1,0:T(8,128)S(1)}, f32[8,128]{1,0:T(8,128)S(1)}, bf16[3456,384]{1,0:T(8,128)(2,1)S(1)}, bf16[...) custom-call(s32[8]{0:T(128)S(1)} %copy-done.5, s32[1]{0:T(128)} %bitcast.position_ref, ...), custom_call_target="tpu_custom_call" | custom-call | bytes 15925248 | tf_op jit(solution)/shard_map/prepare/pallas_call | solution.py:418
  17.4 11.3 %all-to-all-done = bf16[16,64,384]{2,1,0:T(8,128)(2,1)S(1)} async-done(((bf16[16,64,384]{2,1,0:T(8,128)(2,1)}), bf16[16,64,384]{2,1,0:T(8,128)(2,1)S(1)}, u32[]{:S(2)}, u32[]{:S(2)}) %all-to-all-start) | async-done | bytes 786464 | tf_op jit(solution)/shard_map/all_to_all | solution.py:414
  28.7 0.9 %unpack_second.1 = (bf16[256,384]{1,0:T(8,128)(2,1)S(1)}, bf16[256,384]{1,0:T(8,128)(2,1)S(1)}, s32[1,1024]{1,0:T(1,128)S(1)}) custom-call(bf16[1024,384]{1,0:T(8,128)(2,1)S(1)} %bitcast.7, f32[8,768]{1,0:T(8,128)S(1)} %get-tuple-element.28.small_ref), custom_call_target="tpu_custom_call" | custom-call | flops 2038431744 | tf_op jit(solution)/shard_map/unpack_second/pallas_call | solution.py:459
  29.6 0.3 collective-permute-start.1
  29.9 0.6 %unpack_first.1 = (bf16[256,384]{1,0:T(8,128)(2,1)S(1)}, bf16[256,384]{1,0:T(8,128)(2,1)S(1)}) custom-call(bf16[1024,384]{1,0:T(8,128)(2,1)S(1)} %bitcast.8, f32[8,768]{1,0:T(8,128)S(1)} %get-tuple-element.28.small_ref, s32[1,1024]{1,0:T(1,128)S(1)} %get-tuple-element.30.place_ref), custom_call_target="tpu_custom_call" | custom-call | tf_op jit(solution)/shard_map/unpack_first/pallas_call | solution.py:459
  30.5 1.0 %collective-permute-start = (bf16[256,384]{1,0:T(8,128)(2,1)S(1)}, bf16[256,384]{1,0:T(8,128)(2,1)S(1)}, u32[]{:S(2)}, u32[]{:S(2)}) collective-permute-start(bf16[256,384]{1,0:T(8,128)(2,1)S(1)} %get-tuple-element.31.first_ref), channel_id=1, source_target_pairs={{0,1},{1,2},{2,3},{3,4},{4,5},{5,6},{6,7},{7,8},{8,9},{9,10},{10,1... | collective-permute-start | bytes 589832 | tf_op jit(solution)/shard_map/ppermute | solution.py:46
  31.6 0.0 copy-done.1
  31.6 2.4 %local_conv.1 = (f32[256,384]{1,0:T(8,128)S(1)}, f32[256,384]{1,0:T(8,128)S(1)}) custom-call(f32[8,128]{1,0:T(8,128)S(1)} %get-tuple-element.27.keep_ref, bf16[256,384]{1,0:T(8,128)(2,1)S(1)} %get-tuple-element.31.first_ref, bf16[256,384]{1,0:T(8,128)(2,1)S(1)} %get-tuple-element.33.second_ref, bf16[3456,384]{1,0:T(8,128)(2,1)S(1)} %get-tuple-element.34.here_ref, ...), custom_call_target="tpu_custom_call" | custom-call | flops 2038431744 | tf_op jit(solution)/shard_map/local_conv/pallas_call | solution.py:459
  34.0 3.5 %collective-permute-done.1.prior_ref = bf16[256,384]{1,0:T(8,128)(2,1)S(1)} collective-permute-done((bf16[256,384]{1,0:T(8,128)(2,1)S(1)}, bf16[256,384]{1,0:T(8,128)(2,1)S(1)}, u32[]{:S(2)}, u32[]{:S(2)}) %collective-permute-start.1) | collective-permute-done | bytes 196640 | tf_op jit(solution)/shard_map/ppermute | solution.py:46
  37.4 0.0 copy-done
  37.4 0.1 second_residual.1
  37.5 0.1 collective-permute-start.3
  37.6 0.0 copy-start.3
  37.6 0.1 behind.1.sum_ref
  37.7 0.0 copy-start.2
  37.7 1.8 %collective-permute-done.prior_ref = bf16[256,384]{1,0:T(8,128)(2,1)S(1)} collective-permute-done((bf16[256,384]{1,0:T(8,128)(2,1)S(1)}, bf16[256,384]{1,0:T(8,128)(2,1)S(1)}, u32[]{:S(2)}, u32[]{:S(2)}) %collective-permute-start) | collective-permute-done | bytes 196640 | tf_op jit(solution)/shard_map/ppermute | solution.py:46
  39.6 0.5 collective-permute-start.2
  40.1 0.0 copy-done.3
  40.1 0.8 %local_time.1 = (f32[256,768]{1,0:T(8,128)S(1)}, f32[256,768]{1,0:T(8,128)S(1)}) custom-call(f32[8,128]{1,0:T(8,128)S(1)} %get-tuple-element.27.keep_ref, f32[8,768]{1,0:T(8,128)S(1)} %get-tuple-element.28.small_ref, bf16[256,384]{1,0:T(8,128)(2,1)S(1)} %first_residual.1.first_ref, bf16[256,384]{1,0:T(8,128)(2,1)S(1)} %get-tuple-element.41.second_ref, ...), custom_call_target="tpu_custom_call" | custom-call | flops 271790912 | tf_op jit(solution)/shard_map/local_time/pallas_call | solution.py:459
  40.9 0.0 copy-done.2
  40.9 4.5 %early_up.1.early_hbm = bf16[4,32,6144]{2,1,0:T(8,128)(2,1)} custom-call(s32[1]{0:T(128)S(4)} %get-tuple-element.26.solo_ref, f32[8,768]{1,0:T(8,128)S(1)} %get-tuple-element.28.small_ref, f32[256,768]{1,0:T(8,128)S(1)} %get-tuple-element.42.sum0_ref.sum_ref, f32[256,768]{1,0:T(8,128)S(1)} %get-tuple-element.44.sum_ref.sum1_ref, ...), custom_call_target="tpu_custom_call" | custom-call | flops 1358954496 | tf_op jit(solution)/shard_map/early_up/pallas_call | solution.py:459
  45.4 0.0 collective-permute-done.3.prior_ref
  45.4 2.2 %collective-permute-done.2.before_ref = bf16[256,384]{1,0:T(8,128)(2,1)S(1)} collective-permute-done((bf16[256,384]{1,0:T(8,128)(2,1)S(1)}, bf16[256,384]{1,0:T(8,128)(2,1)S(1)}, u32[]{:S(2)}, u32[]{:S(2)}) %collective-permute-start.2) | collective-permute-done | bytes 196640 | tf_op jit(solution)/shard_map/ppermute | solution.py:46
  (14 shorter events, 0.1 us)
Async XLA Ops:
  0.0 10.0 %copy-start.7 = (f32[384]{0:T(512)S(1)}, f32[384]{0:T(512)}, u32[]{:S(2)}) copy-start(f32[384]{0:T(512)} %param.14) | copy-start | bytes 4612
  0.0 10.0 %copy-start.8 = (f32[384]{0:T(512)S(1)}, f32[384]{0:T(512)}, u32[]{:S(2)}) copy-start(f32[384]{0:T(512)} %param.15) | copy-start | bytes 4612
  0.0 10.0 %copy-start.9 = (f32[384]{0:T(512)S(1)}, f32[384]{0:T(512)}, u32[]{:S(2)}) copy-start(f32[384]{0:T(512)} %param.17) | copy-start | bytes 4612
  0.0 10.0 %copy-start.6 = (f32[768]{0:T(1024)S(1)}, f32[768]{0:T(1024)}, u32[]{:S(2)}) copy-start(f32[768]{0:T(1024)} %param.19) | copy-start | bytes 9220
  0.0 10.1 %copy-start.4 = (f32[192]{0:T(256)S(1)}, f32[192]{0:T(256)}, u32[]{:S(2)}) copy-start(f32[192]{0:T(256)} %param.21) | copy-start | bytes 2308
  0.0 10.1 %copy-start.5 = (s32[8]{0:T(128)S(1)}, s32[8]{0:T(128)}, u32[]{:S(2)}) copy-start(s32[8]{0:T(128)} %counts_ref.1) | copy-start | bytes 100
  2.6 26.1 %all-to-all-start = ((bf16[16,64,384]{2,1,0:T(8,128)(2,1)}), bf16[16,64,384]{2,1,0:T(8,128)(2,1)S(1)}, u32[]{:S(2)}, u32[]{:S(2)}) async-start(bf16[16,64,384]{2,1,0:T(8,128)(2,1)} %bitcast.5), calls=%async_computation | async-start | bytes 1572864 | tf_op jit(solution)/shard_map/all_to_all | solution.py:414
  28.7 2.9 %copy-start.1 = (bf16[3456,384]{1,0:T(8,128)(2,1)S(1)}, bf16[3456,384]{1,0:T(8,128)(2,1)}, u32[]{:S(2)}) copy-start(bf16[3456,384]{1,0:T(8,128)(2,1)} %get-tuple-element.35.behind_ref) | copy-start | bytes 7962628
  29.6 7.8 %collective-permute-start.1 = (bf16[256,384]{1,0:T(8,128)(2,1)S(1)}, bf16[256,384]{1,0:T(8,128)(2,1)S(1)}, u32[]{:S(2)}, u32[]{:S(2)}) collective-permute-start(bf16[256,384]{1,0:T(8,128)(2,1)S(1)} %get-tuple-element.33.second_ref), channel_id=1, source_target_pairs={{0,1},{1,2},{2,3},{3,4},{4,5},{5,6},{6,7},{7,8},{8,9},{9,10},{10,1... | collective-permute-start | bytes 589832 | tf_op jit(solution)/shard_map/ppermute | solution.py:46
  30.5 9.0 %collective-permute-start = (bf16[256,384]{1,0:T(8,128)(2,1)S(1)}, bf16[256,384]{1,0:T(8,128)(2,1)S(1)}, u32[]{:S(2)}, u32[]{:S(2)}) collective-permute-start(bf16[256,384]{1,0:T(8,128)(2,1)S(1)} %get-tuple-element.31.first_ref), channel_id=1, source_target_pairs={{0,1},{1,2},{2,3},{3,4},{4,5},{5,6},{6,7},{7,8},{8,9},{9,10},{10,1... | collective-permute-start | bytes 589832 | tf_op jit(solution)/shard_map/ppermute | solution.py:46
  31.6 5.9 %copy-start = (bf16[3456,384]{1,0:T(8,128)(2,1)S(1)}, bf16[3456,384]{1,0:T(8,128)(2,1)}, u32[]{:S(2)}) copy-start(bf16[3456,384]{1,0:T(8,128)(2,1)} %get-tuple-element.32.far_ref) | copy-start | bytes 7962628
  37.5 7.9 %collective-permute-start.3 = (bf16[256,384]{1,0:T(8,128)(2,1)S(1)}, bf16[256,384]{1,0:T(8,128)(2,1)S(1)}, u32[]{:S(2)}, u32[]{:S(2)}) collective-permute-start(bf16[256,384]{1,0:T(8,128)(2,1)S(1)} %get-tuple-element.41.second_ref), channel_id=1, source_target_pairs={{0,1},{1,2},{2,3},{3,4},{4,5},{5,6},{6,7},{7,8},{8,9},{9,10},{10,1... | collective-permute-start | bytes 589832 | tf_op jit(solution)/shard_map/ppermute | solution.py:46
  37.6 2.4 %copy-start.3 = (bf16[3,384,768]{2,1,0:T(8,128)(2,1)S(1)}, bf16[3,384,768]{2,1,0:T(8,128)(2,1)}, u32[]{:S(2)}) copy-start(bf16[3,384,768]{2,1,0:T(8,128)(2,1)} %time_ref.5) | copy-start | bytes 5308420
  37.7 3.1 %copy-start.2 = (bf16[2,3,768,192]{3,2,1,0:T(8,128)(2,1)S(1)}, bf16[2,3,768,192]{3,2,1,0:T(8,128)(2,1)}, u32[]{:S(2)}) copy-start(bf16[2,3,768,192]{3,2,1,0:T(8,128)(2,1)} %get-tuple-element.43.folded_ref) | copy-start | bytes 5308420
  39.6 8.0 %collective-permute-start.2 = (bf16[256,384]{1,0:T(8,128)(2,1)S(1)}, bf16[256,384]{1,0:T(8,128)(2,1)S(1)}, u32[]{:S(2)}, u32[]{:S(2)}) collective-permute-start(bf16[256,384]{1,0:T(8,128)(2,1)S(1)} %first_residual.1.first_ref), channel_id=1, source_target_pairs={{0,1},{1,2},{2,3},{3,4},{4,5},{5,6},{6,7},{7,8},{8,9},{9,10},{10,1... | collective-permute-start | bytes 589832 | tf_op jit(solution)/shard_map/ppermute | solution.py:46
where the time goes:
time: 48.5 us; the launch traced here: 47.8 us
  Pallas kernels  19.4 us (40%)
  waiting for transfers between devices  18.7 us (39%)
  starting transfers between devices  9.26 us (19%)
    all_to_all x1, waiting for transfers between devices, on_device(): lax.all_to_all(packed, 'tm', split_axis=0, concat_axis=0, tiled=True)  11.3 us
    pallas_call x10, Pallas kernels, call(): pl.pallas_call(body, out_shape=outputs, in_specs=in_specs, out_specs=out_...  9.5 us
    ppermute x4, waiting for transfers between devices, from_behind(): return lax.ppermute(value, axis, [(i, (i + 1) % size) for i in range(size)])  7.45 us
    all_to_all x1, starting transfers between devices, on_device(): lax.all_to_all(packed, 'tm', split_axis=0, concat_axis=0, tiled=True)  7.4 us
    pallas_call x1, Pallas kernels, on_device(): pl.pallas_call(prepare_kernel, out_shape=[pltpu.HBM((2, 3, 2 * channels,...  7.32 us
    pallas_call x1, Pallas kernels, on_device(): pl.pallas_call(functools.partial(pack_kernel, peers=peers, capacity=capac...  2.54 us
    ppermute x4, starting transfers between devices, from_behind(): return lax.ppermute(value, axis, [(i, (i + 1) % size) for i in range(size)])  1.86 us
  transfers between devices with their start and end apart: 5, of which 4 were waited for; matrix products, arithmetic and copies ran while one was open for 0% of the time, Pallas kernels for 33%

commit v1 on v0

--- a/solution.py
+++ b/solution.py
@@ -152,7 +152,8 @@
 
 
 def local_conv_kernel(
-    keep_ref, first_ref, second_ref, here_ref, behind_ref, sum0_ref, sum1_ref
+    keep_ref, small_ref, first_ref, second_ref, decoded0_ref, decoded1_ref, here_ref, behind_ref,
+    sum0_ref, sum1_ref,
 ):
     keep = kept(keep_ref)
     channels = sum0_ref.shape[1]
@@ -160,40 +161,36 @@
     both = mm(
         patches(first_ref[...]), jnp.concatenate([here_ref[...], behind_ref[...]], 1)
     )
-    sum0_ref[...] = both[:, :channels]
-    sum1_ref[...] = sum1 + keep[1][1] * both[:, channels:]
+    bias = small_ref[2:3, :channels]
+    sum0_ref[...] = both[:, :channels] + decoded0_ref[...].astype(f32) + bias
+    base = decoded1_ref[...].astype(f32) + bias
+    sum1_ref[...] = sum1 + base + keep[1][1] * both[:, channels:]
 
 
 def second_residual_kernel(
-    solo_ref, keep_ref, small_ref, prior_ref, far_ref, sum_ref, decoded_ref, out_ref, near_ref
-):
-    base = sum_ref[...] + decoded_ref[...].astype(f32) + small_ref[2:3, : out_ref.shape[1]]
-
-
+    solo_ref, keep_ref, prior_ref, far_ref, sum_ref, out_ref, near_ref
+):
     @pl.when(solo_ref[0] == 1)
     def _():
-        out_ref[...] = base.astype(bf16)
+        out_ref[...] = sum_ref[...].astype(bf16)
 
     @pl.when(solo_ref[0] == 0)
     def _():
         near = patches(prior_ref[...])
         near_ref[...] = near
         far = kept(keep_ref)[1][2] * convolve(near, far_ref[...])
-        out_ref[...] = (base + far).astype(bf16)
-
-
-def behind_kernel(
-    solo_ref, keep_ref, small_ref, near_ref, behind_ref, sum_ref, decoded_ref, out_ref
-):
-    base = sum_ref[...] + decoded_ref[...].astype(f32) + small_ref[2:3, : out_ref.shape[1]]
-
+        out_ref[...] = (sum_ref[...] + far).astype(bf16)
+
+
+def behind_kernel(solo_ref, keep_ref, near_ref, behind_ref, sum_ref, out_ref):
     @pl.when(solo_ref[0] == 1)
     def _():
-        out_ref[...] = base
+        out_ref[...] = sum_ref[...]
 
     @pl.when(solo_ref[0] == 0)
     def _():
-        out_ref[...] = base + kept(keep_ref)[0][1] * convolve(near_ref[...], behind_ref[...])
+        behind = convolve(near_ref[...], behind_ref[...])
+        out_ref[...] = sum_ref[...] + kept(keep_ref)[0][1] * behind
 
 
 def first_residual_kernel(solo_ref, keep_ref, prior_ref, far_ref, sum_ref, out_ref):
@@ -225,36 +222,37 @@
     outs = folded_ref.shape[3]
     both = temporal.astype(bf16)
     nothing = jnp.zeros((H, 3 * channels), bf16)
+    bias = small_ref[4:5, :outs]
+    blocks = 2 * outs // 128
+    stride = pixels + 2 * H
     for half in range(2):
-        base = H + half * (pixels + H)
+        base = H + half * stride
         near[base - H : base] = nothing
+        near[base + pixels : base + pixels + H] = nothing
         shown = both[:, half * channels : (half + 1) * channels]
         for t, part in enumerate(steps(shown)):
             near[base : base + pixels, t * channels : (t + 1) * channels] = part
-    near[2 * (H + pixels) :] = nothing
-    span = 2 * pixels + H
-    bias = small_ref[4:5, :outs]
-    blocks = 2 * outs // 128
-    products = []
-    for q in range(2):
-        for t in range(3):
-            windows = [
-                near[(q + side) * H : (q + side) * H + span, t * channels : (t + 1) * channels]
-                for side in range(2)
-            ]
-            products.append(mm(jnp.concatenate(windows, 1), folded_ref[q, t]))
-    for p in range(2):
-        pair = jnp.concatenate(
-            [products[3 * q + 1] + bias + products[3 * q + 2 * p] for q in range(2)], 1
-        )
-        for half in range(2):
+    for half in range(2):
+        products = []
+        for q in range(2):
+            for t in range(3):
+                windows = [
+                    near[
+                        half * stride + (q + side) * H : half * stride + (q + side) * H + pixels,
+                        t * channels : (t + 1) * channels,
+                    ]
+                    for side in range(2)
+                ]
+                products.append(mm(jnp.concatenate(windows, 1), folded_ref[q, t]))
+        for p in range(2):
+            pair = jnp.concatenate(
+                [products[3 * q + 1] + bias + products[3 * q + 2 * p] for q in range(2)], 1
+            )
             for x in range(W):
-                row = half * (pixels + H) + x * H
                 for block in range(blocks):
                     rows32[half, x * blocks + block, pl.ds(p, H, stride=2)] = pair[
-                        row : row + H, block * 128 : (block + 1) * 128
+                        x * H : (x + 1) * H, block * 128 : (block + 1) * 128
                     ]
-    for half in range(2):
         for block in range(W * blocks):
             made_ref[2 * frame + half, :, block * 128 : (block + 1) * 128] = rows32[
                 half, block
@@ -494,15 +492,17 @@
         local_conv_kernel,
         "local_conv",
         [frame32] * 2,
-        [keep, vm(active0), vm(active1), vm(here), behind],
+        [
+            keep, small, vm(active0), vm(active1), vm(decoded0), vm(decoded1), vm(here), behind,
+        ],
         share=3,
     )
     second, near = call(
         second_residual_kernel,
         "second_residual",
         [frame16, near_shape],
-        [solo, keep, small, vm(prior1), far, vm(sum1), vm(decoded1)],
-        in_specs=[SM] + [VM] * 6,
+        [solo, keep, vm(prior1), far, vm(sum1)],
+        in_specs=[SM] + [VM] * 4,
         share=1,
     )
     prior_second = from_behind(second, "tm")
@@ -510,8 +510,8 @@
         behind_kernel,
         "behind",
         [frame32],
-        [solo, keep, small, vm(near), behind, vm(sum0), vm(decoded0)],
-        in_specs=[SM] + [VM] * 6,
+        [solo, keep, vm(near), behind, vm(sum0)],
+        in_specs=[SM] + [VM] * 4,
         share=1,
     )
     (first,) = call(
@@ -534,7 +534,7 @@
     frames = 2 * tokens // pixels
     shape = (frames, 2 * H, 2 * W * outs)
     up_scratch = [
-        pltpu.VMEM((2 * pixels + 3 * H, 3 * channels), bf16),
+        pltpu.VMEM((2 * pixels + 4 * H, 3 * channels), bf16),
         pltpu.VMEM((2, 2 * W * outs // 128, 2 * H, 128), f32),
     ]
     folded, prior_second = vm(folded), vm(prior_second)

time: 48.5 us -> 48.2 us (level)
  waiting for transfers between devices: 18.7 us -> 19.2 us
  transfers between devices with their start and end apart: 5 -> 5, of which waited for: 4 -> 5; matrix products, arithmetic and copies ran while one was open for 0% -> 0% of each run, Pallas kernels for 33% -> 33%
where the time goes in v1:
time: 48.2 us; the launch traced here: 47.7 us
  Pallas kernels  19.2 us (40%)
  waiting for transfers between devices  19.2 us (40%)
  starting transfers between devices  8.84 us (18%)
    all_to_all x1, waiting for transfers between devices, on_device(): lax.all_to_all(packed, 'tm', split_axis=0, concat_axis=0, tiled=True)  11.3 us
    pallas_call x10, Pallas kernels, call(): pl.pallas_call(body, out_shape=outputs, in_specs=in_specs, out_specs=out_...  9.31 us
    ppermute x4, waiting for transfers between devices, from_behind(): return lax.ppermute(value, axis, [(i, (i + 1) % size) for i in range(size)])  7.94 us
    all_to_all x1, starting transfers between devices, on_device(): lax.all_to_all(packed, 'tm', split_axis=0, concat_axis=0, tiled=True)  7.4 us
    pallas_call x1, Pallas kernels, on_device(): pl.pallas_call(prepare_kernel, out_shape=[pltpu.HBM((2, 3, 2 * channels,...  7.32 us
    pallas_call x1, Pallas kernels, on_device(): pl.pallas_call(functools.partial(pack_kernel, peers=peers, capacity=capac...  2.54 us
    ppermute x4, starting transfers between devices, from_behind(): return lax.ppermute(value, axis, [(i, (i + 1) % size) for i in range(size)])  1.44 us
  transfers between devices with their start and end apart: 5, of which 5 were waited for; matrix products, arithmetic and copies ran while one was open for 0% of the time, Pallas kernels for 33%

profile of v1, /device:TPU:0, one launch (start us, length us, event | category | flops | bytes accessed | tf_op | source)
XLA Modules:
  0.0 47.7 jit_solution(11994863266926048402)
XLA Ops:
  0.0 0.0 copy-start.7
  0.0 0.0 copy-start.8
  0.0 0.0 copy-start.5
  0.0 2.5 %pack.1 = bf16[1024,384]{1,0:T(8,128)(2,1)} custom-call(s32[1,512]{1,0:T(1,128)} %bitcast.12, bf16[512,384]{1,0:T(8,128)(2,1)} %latent_hbm.1), custom_call_target="tpu_custom_call" | custom-call | tf_op jit(solution)/shard_map/pack/pallas_call | solution.py:396
  2.6 7.4 %all-to-all-start = ((bf16[16,64,384]{2,1,0:T(8,128)(2,1)}), bf16[16,64,384]{2,1,0:T(8,128)(2,1)S(1)}, u32[]{:S(2)}, u32[]{:S(2)}) async-start(bf16[16,64,384]{2,1,0:T(8,128)(2,1)} %bitcast.5), calls=%async_computation | async-start | bytes 1572864 | tf_op jit(solution)/shard_map/all_to_all | solution.py:412
  10.0 0.0 copy-done.7
  10.0 0.0 copy-done.8
  10.0 0.0 copy-done.9
  10.0 0.0 copy-done.6
  10.1 0.0 copy-done.4
  10.1 0.0 copy-done.5
  10.1 7.3 %prepare.1 = (bf16[2,3,768,192]{3,2,1,0:T(8,128)(2,1)}, f32[8,768]{1,0:T(8,128)S(1)}, f32[8,128]{1,0:T(8,128)S(1)}, bf16[3456,384]{1,0:T(8,128)(2,1)S(1)}, bf16[...) custom-call(s32[8]{0:T(128)S(1)} %copy-done.5, s32[1]{0:T(128)} %bitcast.position_ref, ...), custom_call_target="tpu_custom_call" | custom-call | bytes 15925248 | tf_op jit(solution)/shard_map/prepare/pallas_call | solution.py:416
  17.4 11.3 %all-to-all-done = bf16[16,64,384]{2,1,0:T(8,128)(2,1)S(1)} async-done(((bf16[16,64,384]{2,1,0:T(8,128)(2,1)}), bf16[16,64,384]{2,1,0:T(8,128)(2,1)S(1)}, u32[]{:S(2)}, u32[]{:S(2)}) %all-to-all-start) | async-done | bytes 786464 | tf_op jit(solution)/shard_map/all_to_all | solution.py:412
  28.7 0.9 %unpack_second.1 = (bf16[256,384]{1,0:T(8,128)(2,1)S(1)}, bf16[256,384]{1,0:T(8,128)(2,1)S(1)}, s32[1,1024]{1,0:T(1,128)S(1)}) custom-call(bf16[1024,384]{1,0:T(8,128)(2,1)S(1)} %bitcast.7, f32[8,768]{1,0:T(8,128)S(1)} %get-tuple-element.28.small_ref), custom_call_target="tpu_custom_call" | custom-call | flops 2038431744 | tf_op jit(solution)/shard_map/unpack_second/pallas_call | solution.py:457
  29.6 0.3 collective-permute-start.1
  29.9 0.6 %unpack_first.1 = (bf16[256,384]{1,0:T(8,128)(2,1)S(1)}, bf16[256,384]{1,0:T(8,128)(2,1)S(1)}) custom-call(bf16[1024,384]{1,0:T(8,128)(2,1)S(1)} %bitcast.8, f32[8,768]{1,0:T(8,128)S(1)} %get-tuple-element.28.small_ref, s32[1,1024]{1,0:T(1,128)S(1)} %get-tuple-element.30.place_ref), custom_call_target="tpu_custom_call" | custom-call | tf_op jit(solution)/shard_map/unpack_first/pallas_call | solution.py:457
  30.5 1.0 %collective-permute-start = (bf16[256,384]{1,0:T(8,128)(2,1)S(1)}, bf16[256,384]{1,0:T(8,128)(2,1)S(1)}, u32[]{:S(2)}, u32[]{:S(2)}) collective-permute-start(bf16[256,384]{1,0:T(8,128)(2,1)S(1)} %get-tuple-element.31.first_ref), channel_id=1, source_target_pairs={{0,1},{1,2},{2,3},{3,4},{4,5},{5,6},{6,7},{7,8},{8,9},{9,10},{10,1... | collective-permute-start | bytes 589832 | tf_op jit(solution)/shard_map/ppermute | solution.py:46
  31.6 0.0 copy-done.1
  31.6 2.4 %local_conv.1 = (f32[256,384]{1,0:T(8,128)S(1)}, f32[256,384]{1,0:T(8,128)S(1)}) custom-call(f32[8,128]{1,0:T(8,128)S(1)} %get-tuple-element.27.keep_ref, f32[8,768]{1,0:T(8,128)S(1)} %get-tuple-element.28.small_ref, bf16[256,384]{1,0:T(8,128)(2,1)S(1)} %get-tuple-element.31.first_ref, bf16[256,384]{1,0:T(8,128)(2,1)S(1)} %get-tuple-element.33.second_ref, ...), custom_call_target="tpu_custom_call" | custom-call | flops 2038431744 | tf_op jit(solution)/shard_map/local_conv/pallas_call | solution.py:457
  34.0 3.5 %collective-permute-done.1.prior_ref = bf16[256,384]{1,0:T(8,128)(2,1)S(1)} collective-permute-done((bf16[256,384]{1,0:T(8,128)(2,1)S(1)}, bf16[256,384]{1,0:T(8,128)(2,1)S(1)}, u32[]{:S(2)}, u32[]{:S(2)}) %collective-permute-start.1) | collective-permute-done | bytes 196640 | tf_op jit(solution)/shard_map/ppermute | solution.py:46
  37.4 0.0 copy-done
  37.5 0.1 collective-permute-start.3
  37.5 0.0 copy-start.3
  37.6 0.0 copy-start.2
  37.6 1.9 %collective-permute-done.prior_ref = bf16[256,384]{1,0:T(8,128)(2,1)S(1)} collective-permute-done((bf16[256,384]{1,0:T(8,128)(2,1)S(1)}, bf16[256,384]{1,0:T(8,128)(2,1)S(1)}, u32[]{:S(2)}, u32[]{:S(2)}) %collective-permute-start) | collective-permute-done | bytes 196640 | tf_op jit(solution)/shard_map/ppermute | solution.py:46
  39.6 0.1 collective-permute-start.2
  39.6 0.0 copy-done.3
  39.7 0.8 %local_time.1 = (f32[256,768]{1,0:T(8,128)S(1)}, f32[256,768]{1,0:T(8,128)S(1)}) custom-call(f32[8,128]{1,0:T(8,128)S(1)} %get-tuple-element.27.keep_ref, f32[8,768]{1,0:T(8,128)S(1)} %get-tuple-element.28.small_ref, bf16[256,384]{1,0:T(8,128)(2,1)S(1)} %first_residual.1.first_ref, bf16[256,384]{1,0:T(8,128)(2,1)S(1)} %get-tuple-element.41.second_ref, ...), custom_call_target="tpu_custom_call" | custom-call | flops 271790912 | tf_op jit(solution)/shard_map/local_time/pallas_call | solution.py:457
  40.5 0.0 copy-done.2
  40.5 4.5 %early_up.1.early_hbm = bf16[4,32,6144]{2,1,0:T(8,128)(2,1)} custom-call(s32[1]{0:T(128)S(4)} %get-tuple-element.26.solo_ref, f32[8,768]{1,0:T(8,128)S(1)} %get-tuple-element.28.small_ref, f32[256,768]{1,0:T(8,128)S(1)} %get-tuple-element.42.sum0_ref.sum_ref, f32[256,768]{1,0:T(8,128)S(1)} %get-tuple-element.44.sum_ref.sum1_ref, ...), custom_call_target="tpu_custom_call" | custom-call | flops 1358954496 | tf_op jit(solution)/shard_map/early_up/pallas_call | solution.py:457
  44.9 0.4 collective-permute-done.3.prior_ref
  45.3 2.2 %collective-permute-done.2.before_ref = bf16[256,384]{1,0:T(8,128)(2,1)S(1)} collective-permute-done((bf16[256,384]{1,0:T(8,128)(2,1)S(1)}, bf16[256,384]{1,0:T(8,128)(2,1)S(1)}, u32[]{:S(2)}, u32[]{:S(2)}) %collective-permute-start.2) | collective-permute-done | bytes 196640 | tf_op jit(solution)/shard_map/ppermute | solution.py:46
  (14 shorter events, 0.1 us)
Async XLA Ops:
  0.0 10.0 %copy-start.7 = (f32[384]{0:T(512)S(1)}, f32[384]{0:T(512)}, u32[]{:S(2)}) copy-start(f32[384]{0:T(512)} %param.14) | copy-start | bytes 4612
  0.0 10.0 %copy-start.8 = (f32[384]{0:T(512)S(1)}, f32[384]{0:T(512)}, u32[]{:S(2)}) copy-start(f32[384]{0:T(512)} %param.15) | copy-start | bytes 4612
  0.0 10.0 %copy-start.9 = (f32[384]{0:T(512)S(1)}, f32[384]{0:T(512)}, u32[]{:S(2)}) copy-start(f32[384]{0:T(512)} %param.17) | copy-start | bytes 4612
  0.0 10.0 %copy-start.6 = (f32[768]{0:T(1024)S(1)}, f32[768]{0:T(1024)}, u32[]{:S(2)}) copy-start(f32[768]{0:T(1024)} %param.19) | copy-start | bytes 9220
  0.0 10.1 %copy-start.4 = (f32[192]{0:T(256)S(1)}, f32[192]{0:T(256)}, u32[]{:S(2)}) copy-start(f32[192]{0:T(256)} %param.21) | copy-start | bytes 2308
  0.0 10.1 %copy-start.5 = (s32[8]{0:T(128)S(1)}, s32[8]{0:T(128)}, u32[]{:S(2)}) copy-start(s32[8]{0:T(128)} %counts_ref.1) | copy-start | bytes 100
  2.6 26.1 %all-to-all-start = ((bf16[16,64,384]{2,1,0:T(8,128)(2,1)}), bf16[16,64,384]{2,1,0:T(8,128)(2,1)S(1)}, u32[]{:S(2)}, u32[]{:S(2)}) async-start(bf16[16,64,384]{2,1,0:T(8,128)(2,1)} %bitcast.5), calls=%async_computation | async-start | bytes 1572864 | tf_op jit(solution)/shard_map/all_to_all | solution.py:412
  28.7 2.9 %copy-start.1 = (bf16[3456,384]{1,0:T(8,128)(2,1)S(1)}, bf16[3456,384]{1,0:T(8,128)(2,1)}, u32[]{:S(2)}) copy-start(bf16[3456,384]{1,0:T(8,128)(2,1)} %get-tuple-element.37.behind_ref) | copy-start | bytes 7962628
  29.6 7.8 %collective-permute-start.1 = (bf16[256,384]{1,0:T(8,128)(2,1)S(1)}, bf16[256,384]{1,0:T(8,128)(2,1)S(1)}, u32[]{:S(2)}, u32[]{:S(2)}) collective-permute-start(bf16[256,384]{1,0:T(8,128)(2,1)S(1)} %get-tuple-element.33.second_ref), channel_id=1, source_target_pairs={{0,1},{1,2},{2,3},{3,4},{4,5},{5,6},{6,7},{7,8},{8,9},{9,10},{10,1... | collective-permute-start | bytes 589832 | tf_op jit(solution)/shard_map/ppermute | solution.py:46
  30.5 9.0 %collective-permute-start = (bf16[256,384]{1,0:T(8,128)(2,1)S(1)}, bf16[256,384]{1,0:T(8,128)(2,1)S(1)}, u32[]{:S(2)}, u32[]{:S(2)}) collective-permute-start(bf16[256,384]{1,0:T(8,128)(2,1)S(1)} %get-tuple-element.31.first_ref), channel_id=1, source_target_pairs={{0,1},{1,2},{2,3},{3,4},{4,5},{5,6},{6,7},{7,8},{8,9},{9,10},{10,1... | collective-permute-start | bytes 589832 | tf_op jit(solution)/shard_map/ppermute | solution.py:46
  31.6 5.9 %copy-start = (bf16[3456,384]{1,0:T(8,128)(2,1)S(1)}, bf16[3456,384]{1,0:T(8,128)(2,1)}, u32[]{:S(2)}) copy-start(bf16[3456,384]{1,0:T(8,128)(2,1)} %get-tuple-element.32.far_ref) | copy-start | bytes 7962628
  37.5 7.8 %collective-permute-start.3 = (bf16[256,384]{1,0:T(8,128)(2,1)S(1)}, bf16[256,384]{1,0:T(8,128)(2,1)S(1)}, u32[]{:S(2)}, u32[]{:S(2)}) collective-permute-start(bf16[256,384]{1,0:T(8,128)(2,1)S(1)} %get-tuple-element.41.second_ref), channel_id=1, source_target_pairs={{0,1},{1,2},{2,3},{3,4},{4,5},{5,6},{6,7},{7,8},{8,9},{9,10},{10,1... | collective-permute-start | bytes 589832 | tf_op jit(solution)/shard_map/ppermute | solution.py:46
  37.5 2.1 %copy-start.3 = (bf16[3,384,768]{2,1,0:T(8,128)(2,1)S(1)}, bf16[3,384,768]{2,1,0:T(8,128)(2,1)}, u32[]{:S(2)}) copy-start(bf16[3,384,768]{2,1,0:T(8,128)(2,1)} %time_ref.5) | copy-start | bytes 5308420
  37.6 2.9 %copy-start.2 = (bf16[2,3,768,192]{3,2,1,0:T(8,128)(2,1)S(1)}, bf16[2,3,768,192]{3,2,1,0:T(8,128)(2,1)}, u32[]{:S(2)}) copy-start(bf16[2,3,768,192]{3,2,1,0:T(8,128)(2,1)} %get-tuple-element.43.folded_ref) | copy-start | bytes 5308420
  39.6 7.9 %collective-permute-start.2 = (bf16[256,384]{1,0:T(8,128)(2,1)S(1)}, bf16[256,384]{1,0:T(8,128)(2,1)S(1)}, u32[]{:S(2)}, u32[]{:S(2)}) collective-permute-start(bf16[256,384]{1,0:T(8,128)(2,1)S(1)} %first_residual.1.first_ref), channel_id=1, source_target_pairs={{0,1},{1,2},{2,3},{3,4},{4,5},{5,6},{6,7},{7,8},{8,9},{9,10},{10,1... | collective-permute-start | bytes 589832 | tf_op jit(solution)/shard_map/ppermute | solution.py:46

commit v2 on v1

--- a/solution.py
+++ b/solution.py
@@ -107,7 +107,7 @@
     squares = jnp.mean(values * values, -1, keepdims=True)
     scaled = values * lax.rsqrt(squares + epsilon)
     fed = scaled * small_ref[0:1, :channels] + small_ref[1:2, :channels]
-    active_ref[...] = (fed / (1.0 + jnp.exp(-fed))).astype(bf16)
+    active_ref[...] = (fed * jax.nn.sigmoid(fed)).astype(bf16)
 
 
 def unpack_second_kernel(

time: 48.2 us -> 48 us (level)
  no operation moved by 1% of the time
where the time goes in v2:
time: 48 us; the launch traced here: 47.6 us
  Pallas kernels  19 us (40%)
  waiting for transfers between devices  19 us (40%)
  starting transfers between devices  9.12 us (19%)
    all_to_all x1, waiting for transfers between devices, on_device(): lax.all_to_all(packed, 'tm', split_axis=0, concat_axis=0, tiled=True)  11.3 us
    pallas_call x10, Pallas kernels, call(): pl.pallas_call(body, out_shape=outputs, in_specs=in_specs, out_specs=out_...  9.19 us
    ppermute x4, waiting for transfers between devices, from_behind(): return lax.ppermute(value, axis, [(i, (i + 1) % size) for i in range(size)])  7.68 us
    all_to_all x1, starting transfers between devices, on_device(): lax.all_to_all(packed, 'tm', split_axis=0, concat_axis=0, tiled=True)  7.4 us
    pallas_call x1, Pallas kernels, on_device(): pl.pallas_call(prepare_kernel, out_shape=[pltpu.HBM((2, 3, 2 * channels,...  7.32 us
    pallas_call x1, Pallas kernels, on_device(): pl.pallas_call(functools.partial(pack_kernel, peers=peers, capacity=capac...  2.54 us
    ppermute x4, starting transfers between devices, from_behind(): return lax.ppermute(value, axis, [(i, (i + 1) % size) for i in range(size)])  1.73 us
  transfers between devices with their start and end apart: 5, of which 5 were waited for; matrix products, arithmetic and copies ran while one was open for 0% of the time, Pallas kernels for 33%

profile of v2, /device:TPU:0, one launch (start us, length us, event | category | flops | bytes accessed | tf_op | source)
XLA Modules:
  0.0 47.6 jit_solution(8039624648950568243)
XLA Ops:
  0.0 0.0 copy-start.7
  0.0 0.0 copy-start.8
  0.0 0.0 copy-start.5
  0.0 2.5 %pack.1 = bf16[1024,384]{1,0:T(8,128)(2,1)} custom-call(s32[1,512]{1,0:T(1,128)} %bitcast.12, bf16[512,384]{1,0:T(8,128)(2,1)} %latent_hbm.1), custom_call_target="tpu_custom_call" | custom-call | tf_op jit(solution)/shard_map/pack/pallas_call | solution.py:396
  2.6 7.4 %all-to-all-start = ((bf16[16,64,384]{2,1,0:T(8,128)(2,1)}), bf16[16,64,384]{2,1,0:T(8,128)(2,1)S(1)}, u32[]{:S(2)}, u32[]{:S(2)}) async-start(bf16[16,64,384]{2,1,0:T(8,128)(2,1)} %bitcast.5), calls=%async_computation | async-start | bytes 1572864 | tf_op jit(solution)/shard_map/all_to_all | solution.py:412
  10.0 0.0 copy-done.7
  10.0 0.0 copy-done.8
  10.0 0.0 copy-done.9
  10.0 0.0 copy-done.6
  10.1 0.0 copy-done.4
  10.1 0.0 copy-done.5
  10.1 7.3 %prepare.1 = (bf16[2,3,768,192]{3,2,1,0:T(8,128)(2,1)}, f32[8,768]{1,0:T(8,128)S(1)}, f32[8,128]{1,0:T(8,128)S(1)}, bf16[3456,384]{1,0:T(8,128)(2,1)S(1)}, bf16[...) custom-call(s32[8]{0:T(128)S(1)} %copy-done.5, s32[1]{0:T(128)} %bitcast.position_ref, ...), custom_call_target="tpu_custom_call" | custom-call | bytes 15925248 | tf_op jit(solution)/shard_map/prepare/pallas_call | solution.py:416
  17.4 11.3 %all-to-all-done = bf16[16,64,384]{2,1,0:T(8,128)(2,1)S(1)} async-done(((bf16[16,64,384]{2,1,0:T(8,128)(2,1)}), bf16[16,64,384]{2,1,0:T(8,128)(2,1)S(1)}, u32[]{:S(2)}, u32[]{:S(2)}) %all-to-all-start) | async-done | bytes 786464 | tf_op jit(solution)/shard_map/all_to_all | solution.py:412
  28.7 0.8 %unpack_second.1 = (bf16[256,384]{1,0:T(8,128)(2,1)S(1)}, bf16[256,384]{1,0:T(8,128)(2,1)S(1)}, s32[1,1024]{1,0:T(1,128)S(1)}) custom-call(bf16[1024,384]{1,0:T(8,128)(2,1)S(1)} %bitcast.7, f32[8,768]{1,0:T(8,128)S(1)} %get-tuple-element.28.small_ref), custom_call_target="tpu_custom_call" | custom-call | flops 2038431744 | tf_op jit(solution)/shard_map/unpack_second/pallas_call | solution.py:457
  29.5 0.3 collective-permute-start.1
  29.9 0.6 %unpack_first.1 = (bf16[256,384]{1,0:T(8,128)(2,1)S(1)}, bf16[256,384]{1,0:T(8,128)(2,1)S(1)}) custom-call(bf16[1024,384]{1,0:T(8,128)(2,1)S(1)} %bitcast.8, f32[8,768]{1,0:T(8,128)S(1)} %get-tuple-element.28.small_ref, s32[1,1024]{1,0:T(1,128)S(1)} %get-tuple-element.30.place_ref), custom_call_target="tpu_custom_call" | custom-call | tf_op jit(solution)/shard_map/unpack_first/pallas_call | solution.py:457
  30.4 1.0 %collective-permute-start = (bf16[256,384]{1,0:T(8,128)(2,1)S(1)}, bf16[256,384]{1,0:T(8,128)(2,1)S(1)}, u32[]{:S(2)}, u32[]{:S(2)}) collective-permute-start(bf16[256,384]{1,0:T(8,128)(2,1)S(1)} %get-tuple-element.31.first_ref), channel_id=1, source_target_pairs={{0,1},{1,2},{2,3},{3,4},{4,5},{5,6},{6,7},{7,8},{8,9},{9,10},{10,1... | collective-permute-start | bytes 589832 | tf_op jit(solution)/shard_map/ppermute | solution.py:46
  31.4 0.0 copy-done.1
  31.4 2.4 %local_conv.1 = (f32[256,384]{1,0:T(8,128)S(1)}, f32[256,384]{1,0:T(8,128)S(1)}) custom-call(f32[8,128]{1,0:T(8,128)S(1)} %get-tuple-element.27.keep_ref, f32[8,768]{1,0:T(8,128)S(1)} %get-tuple-element.28.small_ref, bf16[256,384]{1,0:T(8,128)(2,1)S(1)} %get-tuple-element.31.first_ref, bf16[256,384]{1,0:T(8,128)(2,1)S(1)} %get-tuple-element.33.second_ref, ...), custom_call_target="tpu_custom_call" | custom-call | flops 2038431744 | tf_op jit(solution)/shard_map/local_conv/pallas_call | solution.py:457
  33.9 3.5 %collective-permute-done.1.prior_ref = bf16[256,384]{1,0:T(8,128)(2,1)S(1)} collective-permute-done((bf16[256,384]{1,0:T(8,128)(2,1)S(1)}, bf16[256,384]{1,0:T(8,128)(2,1)S(1)}, u32[]{:S(2)}, u32[]{:S(2)}) %collective-permute-start.1) | collective-permute-done | bytes 196640 | tf_op jit(solution)/shard_map/ppermute | solution.py:46
  37.4 0.0 copy-done
  37.4 0.1 collective-permute-start.3
  37.5 0.0 copy-start.3
  37.5 0.0 copy-start.2
  37.6 1.9 %collective-permute-done.prior_ref = bf16[256,384]{1,0:T(8,128)(2,1)S(1)} collective-permute-done((bf16[256,384]{1,0:T(8,128)(2,1)S(1)}, bf16[256,384]{1,0:T(8,128)(2,1)S(1)}, u32[]{:S(2)}, u32[]{:S(2)}) %collective-permute-start) | collective-permute-done | bytes 196640 | tf_op jit(solution)/shard_map/ppermute | solution.py:46
  39.5 0.3 collective-permute-start.2
  39.9 0.0 copy-done.3
  39.9 0.8 %local_time.1 = (f32[256,768]{1,0:T(8,128)S(1)}, f32[256,768]{1,0:T(8,128)S(1)}) custom-call(f32[8,128]{1,0:T(8,128)S(1)} %get-tuple-element.27.keep_ref, f32[8,768]{1,0:T(8,128)S(1)} %get-tuple-element.28.small_ref, bf16[256,384]{1,0:T(8,128)(2,1)S(1)} %first_residual.1.first_ref, bf16[256,384]{1,0:T(8,128)(2,1)S(1)} %get-tuple-element.41.second_ref, ...), custom_call_target="tpu_custom_call" | custom-call | flops 271790912 | tf_op jit(solution)/shard_map/local_time/pallas_call | solution.py:457
  40.7 0.0 copy-done.2
  40.7 4.5 %early_up.1.early_hbm = bf16[4,32,6144]{2,1,0:T(8,128)(2,1)} custom-call(s32[1]{0:T(128)S(4)} %get-tuple-element.26.solo_ref, f32[8,768]{1,0:T(8,128)S(1)} %get-tuple-element.28.small_ref, f32[256,768]{1,0:T(8,128)S(1)} %get-tuple-element.42.sum0_ref.sum_ref, f32[256,768]{1,0:T(8,128)S(1)} %get-tuple-element.44.sum_ref.sum1_ref, ...), custom_call_target="tpu_custom_call" | custom-call | flops 1358954496 | tf_op jit(solution)/shard_map/early_up/pallas_call | solution.py:457
  45.1 0.1 collective-permute-done.3.prior_ref
  45.3 2.1 %collective-permute-done.2.before_ref = bf16[256,384]{1,0:T(8,128)(2,1)S(1)} collective-permute-done((bf16[256,384]{1,0:T(8,128)(2,1)S(1)}, bf16[256,384]{1,0:T(8,128)(2,1)S(1)}, u32[]{:S(2)}, u32[]{:S(2)}) %collective-permute-start.2) | collective-permute-done | bytes 196640 | tf_op jit(solution)/shard_map/ppermute | solution.py:46
  (14 shorter events, 0.1 us)
Async XLA Ops:
  0.0 10.0 %copy-start.7 = (f32[384]{0:T(512)S(1)}, f32[384]{0:T(512)}, u32[]{:S(2)}) copy-start(f32[384]{0:T(512)} %param.14) | copy-start | bytes 4612
  0.0 10.0 %copy-start.8 = (f32[384]{0:T(512)S(1)}, f32[384]{0:T(512)}, u32[]{:S(2)}) copy-start(f32[384]{0:T(512)} %param.15) | copy-start | bytes 4612
  0.0 10.0 %copy-start.9 = (f32[384]{0:T(512)S(1)}, f32[384]{0:T(512)}, u32[]{:S(2)}) copy-start(f32[384]{0:T(512)} %param.17) | copy-start | bytes 4612
  0.0 10.0 %copy-start.6 = (f32[768]{0:T(1024)S(1)}, f32[768]{0:T(1024)}, u32[]{:S(2)}) copy-start(f32[768]{0:T(1024)} %param.19) | copy-start | bytes 9220
  0.0 10.1 %copy-start.4 = (f32[192]{0:T(256)S(1)}, f32[192]{0:T(256)}, u32[]{:S(2)}) copy-start(f32[192]{0:T(256)} %param.21) | copy-start | bytes 2308
  0.0 10.1 %copy-start.5 = (s32[8]{0:T(128)S(1)}, s32[8]{0:T(128)}, u32[]{:S(2)}) copy-start(s32[8]{0:T(128)} %counts_ref.1) | copy-start | bytes 100
  2.6 26.1 %all-to-all-start = ((bf16[16,64,384]{2,1,0:T(8,128)(2,1)}), bf16[16,64,384]{2,1,0:T(8,128)(2,1)S(1)}, u32[]{:S(2)}, u32[]{:S(2)}) async-start(bf16[16,64,384]{2,1,0:T(8,128)(2,1)} %bitcast.5), calls=%async_computation | async-start | bytes 1572864 | tf_op jit(solution)/shard_map/all_to_all | solution.py:412
  28.7 2.8 %copy-start.1 = (bf16[3456,384]{1,0:T(8,128)(2,1)S(1)}, bf16[3456,384]{1,0:T(8,128)(2,1)}, u32[]{:S(2)}) copy-start(bf16[3456,384]{1,0:T(8,128)(2,1)} %get-tuple-element.37.behind_ref) | copy-start | bytes 7962628
  29.5 7.8 %collective-permute-start.1 = (bf16[256,384]{1,0:T(8,128)(2,1)S(1)}, bf16[256,384]{1,0:T(8,128)(2,1)S(1)}, u32[]{:S(2)}, u32[]{:S(2)}) collective-permute-start(bf16[256,384]{1,0:T(8,128)(2,1)S(1)} %get-tuple-element.33.second_ref), channel_id=1, source_target_pairs={{0,1},{1,2},{2,3},{3,4},{4,5},{5,6},{6,7},{7,8},{8,9},{9,10},{10,1... | collective-permute-start | bytes 589832 | tf_op jit(solution)/shard_map/ppermute | solution.py:46
  30.4 9.1 %collective-permute-start = (bf16[256,384]{1,0:T(8,128)(2,1)S(1)}, bf16[256,384]{1,0:T(8,128)(2,1)S(1)}, u32[]{:S(2)}, u32[]{:S(2)}) collective-permute-start(bf16[256,384]{1,0:T(8,128)(2,1)S(1)} %get-tuple-element.31.first_ref), channel_id=1, source_target_pairs={{0,1},{1,2},{2,3},{3,4},{4,5},{5,6},{6,7},{7,8},{8,9},{9,10},{10,1... | collective-permute-start | bytes 589832 | tf_op jit(solution)/shard_map/ppermute | solution.py:46
  31.4 5.9 %copy-start = (bf16[3456,384]{1,0:T(8,128)(2,1)S(1)}, bf16[3456,384]{1,0:T(8,128)(2,1)}, u32[]{:S(2)}) copy-start(bf16[3456,384]{1,0:T(8,128)(2,1)} %get-tuple-element.32.far_ref) | copy-start | bytes 7962628
  37.4 7.8 %collective-permute-start.3 = (bf16[256,384]{1,0:T(8,128)(2,1)S(1)}, bf16[256,384]{1,0:T(8,128)(2,1)S(1)}, u32[]{:S(2)}, u32[]{:S(2)}) collective-permute-start(bf16[256,384]{1,0:T(8,128)(2,1)S(1)} %get-tuple-element.41.second_ref), channel_id=1, source_target_pairs={{0,1},{1,2},{2,3},{3,4},{4,5},{5,6},{6,7},{7,8},{8,9},{9,10},{10,1... | collective-permute-start | bytes 589832 | tf_op jit(solution)/shard_map/ppermute | solution.py:46
  37.5 2.4 %copy-start.3 = (bf16[3,384,768]{2,1,0:T(8,128)(2,1)S(1)}, bf16[3,384,768]{2,1,0:T(8,128)(2,1)}, u32[]{:S(2)}) copy-start(bf16[3,384,768]{2,1,0:T(8,128)(2,1)} %time_ref.5) | copy-start | bytes 5308420
  37.5 3.1 %copy-start.2 = (bf16[2,3,768,192]{3,2,1,0:T(8,128)(2,1)S(1)}, bf16[2,3,768,192]{3,2,1,0:T(8,128)(2,1)}, u32[]{:S(2)}) copy-start(bf16[2,3,768,192]{3,2,1,0:T(8,128)(2,1)} %get-tuple-element.43.folded_ref) | copy-start | bytes 5308420
  39.5 7.8 %collective-permute-start.2 = (bf16[256,384]{1,0:T(8,128)(2,1)S(1)}, bf16[256,384]{1,0:T(8,128)(2,1)S(1)}, u32[]{:S(2)}, u32[]{:S(2)}) collective-permute-start(bf16[256,384]{1,0:T(8,128)(2,1)S(1)} %first_residual.1.first_ref), channel_id=1, source_target_pairs={{0,1},{1,2},{2,3},{3,4},{4,5},{5,6},{6,7},{7,8},{8,9},{9,10},{10,1... | collective-permute-start | bytes 589832 | tf_op jit(solution)/shard_map/ppermute | solution.py:46

commit v3 on v2

--- a/solution.py
+++ b/solution.py
@@ -167,29 +167,25 @@
     sum1_ref[...] = sum1 + base + keep[1][1] * both[:, channels:]
 
 
-def second_residual_kernel(
-    solo_ref, keep_ref, prior_ref, far_ref, sum_ref, out_ref, near_ref
-):
+def second_residual_kernel(solo_ref, keep_ref, prior_ref, far_ref, sum_ref, out_ref):
     @pl.when(solo_ref[0] == 1)
     def _():
         out_ref[...] = sum_ref[...].astype(bf16)
 
     @pl.when(solo_ref[0] == 0)
     def _():
-        near = patches(prior_ref[...])
-        near_ref[...] = near
-        far = kept(keep_ref)[1][2] * convolve(near, far_ref[...])
+        far = kept(keep_ref)[1][2] * convolve(patches(prior_ref[...]), far_ref[...])
         out_ref[...] = (sum_ref[...] + far).astype(bf16)
 
 
-def behind_kernel(solo_ref, keep_ref, near_ref, behind_ref, sum_ref, out_ref):
+def behind_kernel(solo_ref, keep_ref, prior_ref, behind_ref, sum_ref, out_ref):
     @pl.when(solo_ref[0] == 1)
     def _():
         out_ref[...] = sum_ref[...]
 
     @pl.when(solo_ref[0] == 0)
     def _():
-        behind = convolve(near_ref[...], behind_ref[...])
+        behind = convolve(patches(prior_ref[...]), behind_ref[...])
         out_ref[...] = sum_ref[...] + kept(keep_ref)[0][1] * behind
 
 
@@ -471,7 +467,6 @@
     vm = in_vmem
     frame16 = pltpu.VMEM((pixels, channels), bf16)
     frame32 = pltpu.VMEM((pixels, channels), f32)
-    near_shape = pltpu.VMEM((pixels, 9 * channels), bf16)
     tap = 2 * pixels * 9 * channels * channels
     sem = pltpu.SemaphoreType.DMA
     small, keep, received = vm(small), vm(keep), vm(received)
@@ -497,11 +492,12 @@
         ],
         share=3,
     )
-    second, near = call(
+    prior1 = vm(prior1)
+    (second,) = call(
         second_residual_kernel,
         "second_residual",
-        [frame16, near_shape],
-        [solo, keep, vm(prior1), far, vm(sum1)],
+        [frame16],
+        [solo, keep, prior1, far, vm(sum1)],
         in_specs=[SM] + [VM] * 4,
         share=1,
     )
@@ -510,7 +506,7 @@
         behind_kernel,
         "behind",
         [frame32],
-        [solo, keep, vm(near), behind, vm(sum0)],
+        [solo, keep, prior1, behind, vm(sum0)],
         in_specs=[SM] + [VM] * 4,
         share=1,
     )

time: 48 us -> 47.9 us (level)
  no operation moved by 1% of the time
where the time goes in v3:
time: 47.9 us; the launch traced here: 47.6 us
  waiting for transfers between devices  19.1 us (40%)
  Pallas kernels  19 us (40%)
  starting transfers between devices  9.03 us (19%)
    all_to_all x1, waiting for transfers between devices, on_device(): lax.all_to_all(packed, 'tm', split_axis=0, concat_axis=0, tiled=True)  11.3 us
    pallas_call x10, Pallas kernels, call(): pl.pallas_call(body, out_shape=outputs, in_specs=in_specs, out_specs=out_...  9.18 us
    ppermute x4, waiting for transfers between devices, from_behind(): return lax.ppermute(value, axis, [(i, (i + 1) % size) for i in range(size)])  7.79 us
    all_to_all x1, starting transfers between devices, on_device(): lax.all_to_all(packed, 'tm', split_axis=0, concat_axis=0, tiled=True)  7.4 us
    pallas_call x1, Pallas kernels, on_device(): pl.pallas_call(prepare_kernel, out_shape=[pltpu.HBM((2, 3, 2 * channels,...  7.32 us
    pallas_call x1, Pallas kernels, on_device(): pl.pallas_call(functools.partial(pack_kernel, peers=peers, capacity=capac...  2.54 us
    ppermute x4, starting transfers between devices, from_behind(): return lax.ppermute(value, axis, [(i, (i + 1) % size) for i in range(size)])  1.63 us
  transfers between devices with their start and end apart: 5, of which 5 were waited for; matrix products, arithmetic and copies ran while one was open for 0% of the time, Pallas kernels for 33%

profile of v3, /device:TPU:0, one launch (start us, length us, event | category | flops | bytes accessed | tf_op | source)
XLA Modules:
  0.0 47.6 jit_solution(11548224823288463175)
XLA Ops:
  0.0 0.0 copy-start.7
  0.0 0.0 copy-start.8
  0.0 0.0 copy-start.5
  0.0 2.5 %pack.1 = bf16[1024,384]{1,0:T(8,128)(2,1)} custom-call(s32[1,512]{1,0:T(1,128)} %bitcast.12, bf16[512,384]{1,0:T(8,128)(2,1)} %latent_hbm.1), custom_call_target="tpu_custom_call" | custom-call | tf_op jit(solution)/shard_map/pack/pallas_call | solution.py:392
  2.6 7.4 %all-to-all-start = ((bf16[16,64,384]{2,1,0:T(8,128)(2,1)}), bf16[16,64,384]{2,1,0:T(8,128)(2,1)S(1)}, u32[]{:S(2)}, u32[]{:S(2)}) async-start(bf16[16,64,384]{2,1,0:T(8,128)(2,1)} %bitcast.5), calls=%async_computation | async-start | bytes 1572864 | tf_op jit(solution)/shard_map/all_to_all | solution.py:408
  10.0 0.0 copy-done.7
  10.0 0.0 copy-done.8
  10.0 0.0 copy-done.9
  10.0 0.0 copy-done.6
  10.1 0.0 copy-done.4
  10.1 0.0 copy-done.5
  10.1 7.3 %prepare.1 = (bf16[2,3,768,192]{3,2,1,0:T(8,128)(2,1)}, f32[8,768]{1,0:T(8,128)S(1)}, f32[8,128]{1,0:T(8,128)S(1)}, bf16[3456,384]{1,0:T(8,128)(2,1)S(1)}, bf16[...) custom-call(s32[8]{0:T(128)S(1)} %copy-done.5, s32[1]{0:T(128)} %bitcast.position_ref, ...), custom_call_target="tpu_custom_call" | custom-call | bytes 15925248 | tf_op jit(solution)/shard_map/prepare/pallas_call | solution.py:412
  17.4 11.3 %all-to-all-done = bf16[16,64,384]{2,1,0:T(8,128)(2,1)S(1)} async-done(((bf16[16,64,384]{2,1,0:T(8,128)(2,1)}), bf16[16,64,384]{2,1,0:T(8,128)(2,1)S(1)}, u32[]{:S(2)}, u32[]{:S(2)}) %all-to-all-start) | async-done | bytes 786464 | tf_op jit(solution)/shard_map/all_to_all | solution.py:408
  28.7 0.8 %unpack_second.1 = (bf16[256,384]{1,0:T(8,128)(2,1)S(1)}, bf16[256,384]{1,0:T(8,128)(2,1)S(1)}, s32[1,1024]{1,0:T(1,128)S(1)}) custom-call(bf16[1024,384]{1,0:T(8,128)(2,1)S(1)} %bitcast.7, f32[8,768]{1,0:T(8,128)S(1)} %get-tuple-element.26.small_ref), custom_call_target="tpu_custom_call" | custom-call | flops 2038431744 | tf_op jit(solution)/shard_map/unpack_second/pallas_call | solution.py:453
  29.5 0.3 collective-permute-start.1
  29.9 0.6 %unpack_first.1 = (bf16[256,384]{1,0:T(8,128)(2,1)S(1)}, bf16[256,384]{1,0:T(8,128)(2,1)S(1)}) custom-call(bf16[1024,384]{1,0:T(8,128)(2,1)S(1)} %bitcast.8, f32[8,768]{1,0:T(8,128)S(1)} %get-tuple-element.26.small_ref, s32[1,1024]{1,0:T(1,128)S(1)} %get-tuple-element.28.place_ref), custom_call_target="tpu_custom_call" | custom-call | tf_op jit(solution)/shard_map/unpack_first/pallas_call | solution.py:453
  30.4 1.0 %collective-permute-start = (bf16[256,384]{1,0:T(8,128)(2,1)S(1)}, bf16[256,384]{1,0:T(8,128)(2,1)S(1)}, u32[]{:S(2)}, u32[]{:S(2)}) collective-permute-start(bf16[256,384]{1,0:T(8,128)(2,1)S(1)} %get-tuple-element.29.first_ref), channel_id=1, source_target_pairs={{0,1},{1,2},{2,3},{3,4},{4,5},{5,6},{6,7},{7,8},{8,9},{9,10},{10,1... | collective-permute-start | bytes 589832 | tf_op jit(solution)/shard_map/ppermute | solution.py:46
  31.4 0.0 copy-done.1
  31.4 2.4 %local_conv.1 = (f32[256,384]{1,0:T(8,128)S(1)}, f32[256,384]{1,0:T(8,128)S(1)}) custom-call(f32[8,128]{1,0:T(8,128)S(1)} %get-tuple-element.25.keep_ref, f32[8,768]{1,0:T(8,128)S(1)} %get-tuple-element.26.small_ref, bf16[256,384]{1,0:T(8,128)(2,1)S(1)} %get-tuple-element.29.first_ref, bf16[256,384]{1,0:T(8,128)(2,1)S(1)} %get-tuple-element.31.second_ref, ...), custom_call_target="tpu_custom_call" | custom-call | flops 2038431744 | tf_op jit(solution)/shard_map/local_conv/pallas_call | solution.py:453
  33.9 3.5 %collective-permute-done.1.prior_ref = bf16[256,384]{1,0:T(8,128)(2,1)S(1)} collective-permute-done((bf16[256,384]{1,0:T(8,128)(2,1)S(1)}, bf16[256,384]{1,0:T(8,128)(2,1)S(1)}, u32[]{:S(2)}, u32[]{:S(2)}) %collective-permute-start.1) | collective-permute-done | bytes 196640 | tf_op jit(solution)/shard_map/ppermute | solution.py:46
  37.4 0.0 copy-done
  37.4 0.1 collective-permute-start.3
  37.5 0.0 copy-start.3
  37.5 0.0 copy-start.2
  37.6 1.9 %collective-permute-done.prior_ref = bf16[256,384]{1,0:T(8,128)(2,1)S(1)} collective-permute-done((bf16[256,384]{1,0:T(8,128)(2,1)S(1)}, bf16[256,384]{1,0:T(8,128)(2,1)S(1)}, u32[]{:S(2)}, u32[]{:S(2)}) %collective-permute-start) | collective-permute-done | bytes 196640 | tf_op jit(solution)/shard_map/ppermute | solution.py:46
  39.5 0.2 collective-permute-start.2
  39.8 0.0 copy-done.3
  39.8 0.8 %local_time.1 = (f32[256,768]{1,0:T(8,128)S(1)}, f32[256,768]{1,0:T(8,128)S(1)}) custom-call(f32[8,128]{1,0:T(8,128)S(1)} %get-tuple-element.25.keep_ref, f32[8,768]{1,0:T(8,128)S(1)} %get-tuple-element.26.small_ref, bf16[256,384]{1,0:T(8,128)(2,1)S(1)} %first_residual.1.first_ref, bf16[256,384]{1,0:T(8,128)(2,1)S(1)} %second_residual.1.second_ref, ...), custom_call_target="tpu_custom_call" | custom-call | flops 271790912 | tf_op jit(solution)/shard_map/local_time/pallas_call | solution.py:453
  40.6 0.0 copy-done.2
  40.6 4.5 %early_up.1.early_hbm = bf16[4,32,6144]{2,1,0:T(8,128)(2,1)} custom-call(s32[1]{0:T(128)S(4)} %get-tuple-element.24.solo_ref, f32[8,768]{1,0:T(8,128)S(1)} %get-tuple-element.26.small_ref, f32[256,768]{1,0:T(8,128)S(1)} %get-tuple-element.38.sum0_ref.sum_ref, f32[256,768]{1,0:T(8,128)S(1)} %get-tuple-element.40.sum_ref.sum1_ref, ...), custom_call_target="tpu_custom_call" | custom-call | flops 1358954496 | tf_op jit(solution)/shard_map/early_up/pallas_call | solution.py:453
  45.0 0.2 collective-permute-done.3.prior_ref
  45.3 2.1 %collective-permute-done.2.before_ref = bf16[256,384]{1,0:T(8,128)(2,1)S(1)} collective-permute-done((bf16[256,384]{1,0:T(8,128)(2,1)S(1)}, bf16[256,384]{1,0:T(8,128)(2,1)S(1)}, u32[]{:S(2)}, u32[]{:S(2)}) %collective-permute-start.2) | collective-permute-done | bytes 196640 | tf_op jit(solution)/shard_map/ppermute | solution.py:46
  (14 shorter events, 0.1 us)
Async XLA Ops:
  0.0 10.0 %copy-start.7 = (f32[384]{0:T(512)S(1)}, f32[384]{0:T(512)}, u32[]{:S(2)}) copy-start(f32[384]{0:T(512)} %param.14) | copy-start | bytes 4612
  0.0 10.0 %copy-start.8 = (f32[384]{0:T(512)S(1)}, f32[384]{0:T(512)}, u32[]{:S(2)}) copy-start(f32[384]{0:T(512)} %param.15) | copy-start | bytes 4612
  0.0 10.0 %copy-start.9 = (f32[384]{0:T(512)S(1)}, f32[384]{0:T(512)}, u32[]{:S(2)}) copy-start(f32[384]{0:T(512)} %param.17) | copy-start | bytes 4612
  0.0 10.0 %copy-start.6 = (f32[768]{0:T(1024)S(1)}, f32[768]{0:T(1024)}, u32[]{:S(2)}) copy-start(f32[768]{0:T(1024)} %param.19) | copy-start | bytes 9220
  0.0 10.1 %copy-start.4 = (f32[192]{0:T(256)S(1)}, f32[192]{0:T(256)}, u32[]{:S(2)}) copy-start(f32[192]{0:T(256)} %param.21) | copy-start | bytes 2308
  0.0 10.1 %copy-start.5 = (s32[8]{0:T(128)S(1)}, s32[8]{0:T(128)}, u32[]{:S(2)}) copy-start(s32[8]{0:T(128)} %counts_ref.1) | copy-start | bytes 100
  2.6 26.1 %all-to-all-start = ((bf16[16,64,384]{2,1,0:T(8,128)(2,1)}), bf16[16,64,384]{2,1,0:T(8,128)(2,1)S(1)}, u32[]{:S(2)}, u32[]{:S(2)}) async-start(bf16[16,64,384]{2,1,0:T(8,128)(2,1)} %bitcast.5), calls=%async_computation | async-start | bytes 1572864 | tf_op jit(solution)/shard_map/all_to_all | solution.py:408
  28.7 2.8 %copy-start.1 = (bf16[3456,384]{1,0:T(8,128)(2,1)S(1)}, bf16[3456,384]{1,0:T(8,128)(2,1)}, u32[]{:S(2)}) copy-start(bf16[3456,384]{1,0:T(8,128)(2,1)} %get-tuple-element.32.behind_ref) | copy-start | bytes 7962628
  29.5 7.8 %collective-permute-start.1 = (bf16[256,384]{1,0:T(8,128)(2,1)S(1)}, bf16[256,384]{1,0:T(8,128)(2,1)S(1)}, u32[]{:S(2)}, u32[]{:S(2)}) collective-permute-start(bf16[256,384]{1,0:T(8,128)(2,1)S(1)} %get-tuple-element.31.second_ref), channel_id=1, source_target_pairs={{0,1},{1,2},{2,3},{3,4},{4,5},{5,6},{6,7},{7,8},{8,9},{9,10},{10,1... | collective-permute-start | bytes 589832 | tf_op jit(solution)/shard_map/ppermute | solution.py:46
  30.4 9.1 %collective-permute-start = (bf16[256,384]{1,0:T(8,128)(2,1)S(1)}, bf16[256,384]{1,0:T(8,128)(2,1)S(1)}, u32[]{:S(2)}, u32[]{:S(2)}) collective-permute-start(bf16[256,384]{1,0:T(8,128)(2,1)S(1)} %get-tuple-element.29.first_ref), channel_id=1, source_target_pairs={{0,1},{1,2},{2,3},{3,4},{4,5},{5,6},{6,7},{7,8},{8,9},{9,10},{10,1... | collective-permute-start | bytes 589832 | tf_op jit(solution)/shard_map/ppermute | solution.py:46
  31.4 5.9 %copy-start = (bf16[3456,384]{1,0:T(8,128)(2,1)S(1)}, bf16[3456,384]{1,0:T(8,128)(2,1)}, u32[]{:S(2)}) copy-start(bf16[3456,384]{1,0:T(8,128)(2,1)} %get-tuple-element.30.far_ref) | copy-start | bytes 7962628
  37.4 7.8 %collective-permute-start.3 = (bf16[256,384]{1,0:T(8,128)(2,1)S(1)}, bf16[256,384]{1,0:T(8,128)(2,1)S(1)}, u32[]{:S(2)}, u32[]{:S(2)}) collective-permute-start(bf16[256,384]{1,0:T(8,128)(2,1)S(1)} %second_residual.1.second_ref), channel_id=1, source_target_pairs={{0,1},{1,2},{2,3},{3,4},{4,5},{5,6},{6,7},{7,8},{8,9},{9,10},{10,1... | collective-permute-start | bytes 589832 | tf_op jit(solution)/shard_map/ppermute | solution.py:46
  37.5 2.3 %copy-start.3 = (bf16[3,384,768]{2,1,0:T(8,128)(2,1)S(1)}, bf16[3,384,768]{2,1,0:T(8,128)(2,1)}, u32[]{:S(2)}) copy-start(bf16[3,384,768]{2,1,0:T(8,128)(2,1)} %time_ref.5) | copy-start | bytes 5308420
  37.5 3.0 %copy-start.2 = (bf16[2,3,768,192]{3,2,1,0:T(8,128)(2,1)S(1)}, bf16[2,3,768,192]{3,2,1,0:T(8,128)(2,1)}, u32[]{:S(2)}) copy-start(bf16[2,3,768,192]{3,2,1,0:T(8,128)(2,1)} %get-tuple-element.39.folded_ref) | copy-start | bytes 5308420
  39.5 7.8 %collective-permute-start.2 = (bf16[256,384]{1,0:T(8,128)(2,1)S(1)}, bf16[256,384]{1,0:T(8,128)(2,1)S(1)}, u32[]{:S(2)}, u32[]{:S(2)}) collective-permute-start(bf16[256,384]{1,0:T(8,128)(2,1)S(1)} %first_residual.1.first_ref), channel_id=1, source_target_pairs={{0,1},{1,2},{2,3},{3,4},{4,5},{5,6},{6,7},{7,8},{8,9},{9,10},{10,1... | collective-permute-start | bytes 589832 | tf_op jit(solution)/shard_map/ppermute | solution.py:46

commit v4 on v3

--- a/solution.py
+++ b/solution.py
@@ -99,15 +99,16 @@
 def unpack(place, got_ref, small_ref, decoded_ref, active_ref, frame):
     slots, channels = got_ref.shape
     pixels = decoded_ref.shape[0]
-    pixel = iota((pixels, slots), 0)
-    source = frame * pixels + (pixel % H) * W + pixel // H
-    chosen = (source == place).astype(bf16)
-    values = mm(chosen, got_ref[...])
-    decoded_ref[...] = values.astype(bf16)
-    squares = jnp.mean(values * values, -1, keepdims=True)
-    scaled = values * lax.rsqrt(squares + epsilon)
-    fed = scaled * small_ref[0:1, :channels] + small_ref[1:2, :channels]
-    active_ref[...] = (fed * jax.nn.sigmoid(fed)).astype(bf16)
+    part = pixels // 2
+    for rows in (slice(0, part), slice(part, pixels)):
+        pixel = iota((part, slots), 0) + rows.start
+        source = frame * pixels + (pixel % H) * W + pixel // H
+        values = mm((source == place).astype(bf16), got_ref[...])
+        decoded_ref[rows] = values.astype(bf16)
+        squares = jnp.mean(values * values, -1, keepdims=True)
+        scaled = values * lax.rsqrt(squares + epsilon)
+        fed = scaled * small_ref[0:1, :channels] + small_ref[1:2, :channels]
+        active_ref[rows] = (fed * jax.nn.sigmoid(fed)).astype(bf16)
 
 
 def unpack_second_kernel(

time: 47.9 us -> 47.9 us (level)
  no operation moved by 1% of the time
where the time goes in v4:
time: 47.9 us; the launch traced here: 47.5 us
  waiting for transfers between devices  19.1 us (40%)
  Pallas kernels  19 us (40%)
  starting transfers between devices  9 us (19%)
    all_to_all x1, waiting for transfers between devices, on_device(): lax.all_to_all(packed, 'tm', split_axis=0, concat_axis=0, tiled=True)  11.3 us
    pallas_call x10, Pallas kernels, call(): pl.pallas_call(body, out_shape=outputs, in_specs=in_specs, out_specs=out_...  9.15 us
    ppermute x4, waiting for transfers between devices, from_behind(): return lax.ppermute(value, axis, [(i, (i + 1) % size) for i in range(size)])  7.83 us
    all_to_all x1, starting transfers between devices, on_device(): lax.all_to_all(packed, 'tm', split_axis=0, concat_axis=0, tiled=True)  7.4 us
    pallas_call x1, Pallas kernels, on_device(): pl.pallas_call(prepare_kernel, out_shape=[pltpu.HBM((2, 3, 2 * channels,...  7.32 us
    pallas_call x1, Pallas kernels, on_device(): pl.pallas_call(functools.partial(pack_kernel, peers=peers, capacity=capac...  2.54 us
    ppermute x4, starting transfers between devices, from_behind(): return lax.ppermute(value, axis, [(i, (i + 1) % size) for i in range(size)])  1.6 us
  transfers between devices with their start and end apart: 5, of which 5 were waited for; matrix products, arithmetic and copies ran while one was open for 0% of the time, Pallas kernels for 33%

profile of v4, /device:TPU:0, one launch (start us, length us, event | category | flops | bytes accessed | tf_op | source)
XLA Modules:
  0.0 47.5 jit_solution(11967320706760454867)
XLA Ops:
  0.0 0.0 copy-start.7
  0.0 0.0 copy-start.8
  0.0 0.0 copy-start.5
  0.0 2.5 %pack.1 = bf16[1024,384]{1,0:T(8,128)(2,1)} custom-call(s32[1,512]{1,0:T(1,128)} %bitcast.12, bf16[512,384]{1,0:T(8,128)(2,1)} %latent_hbm.1), custom_call_target="tpu_custom_call" | custom-call | tf_op jit(solution)/shard_map/pack/pallas_call | solution.py:393
  2.6 7.4 %all-to-all-start = ((bf16[16,64,384]{2,1,0:T(8,128)(2,1)}), bf16[16,64,384]{2,1,0:T(8,128)(2,1)S(1)}, u32[]{:S(2)}, u32[]{:S(2)}) async-start(bf16[16,64,384]{2,1,0:T(8,128)(2,1)} %bitcast.5), calls=%async_computation | async-start | bytes 1572864 | tf_op jit(solution)/shard_map/all_to_all | solution.py:409
  10.0 0.0 copy-done.7
  10.0 0.0 copy-done.8
  10.0 0.0 copy-done.9
  10.0 0.0 copy-done.6
  10.1 0.0 copy-done.4
  10.1 0.0 copy-done.5
  10.1 7.3 %prepare.1 = (bf16[2,3,768,192]{3,2,1,0:T(8,128)(2,1)}, f32[8,768]{1,0:T(8,128)S(1)}, f32[8,128]{1,0:T(8,128)S(1)}, bf16[3456,384]{1,0:T(8,128)(2,1)S(1)}, bf16[...) custom-call(s32[8]{0:T(128)S(1)} %copy-done.5, s32[1]{0:T(128)} %bitcast.position_ref, ...), custom_call_target="tpu_custom_call" | custom-call | bytes 15925248 | tf_op jit(solution)/shard_map/prepare/pallas_call | solution.py:413
  17.4 11.3 %all-to-all-done = bf16[16,64,384]{2,1,0:T(8,128)(2,1)S(1)} async-done(((bf16[16,64,384]{2,1,0:T(8,128)(2,1)}), bf16[16,64,384]{2,1,0:T(8,128)(2,1)S(1)}, u32[]{:S(2)}, u32[]{:S(2)}) %all-to-all-start) | async-done | bytes 786464 | tf_op jit(solution)/shard_map/all_to_all | solution.py:409
  28.7 0.8 %unpack_second.1 = (bf16[256,384]{1,0:T(8,128)(2,1)S(1)}, bf16[256,384]{1,0:T(8,128)(2,1)S(1)}, s32[1,1024]{1,0:T(1,128)S(1)}) custom-call(bf16[1024,384]{1,0:T(8,128)(2,1)S(1)} %bitcast.7, f32[8,768]{1,0:T(8,128)S(1)} %get-tuple-element.26.small_ref), custom_call_target="tpu_custom_call" | custom-call | flops 2038431744 | tf_op jit(solution)/shard_map/unpack_second/pallas_call | solution.py:454
  29.5 0.3 collective-permute-start.1
  29.8 0.5 %unpack_first.1 = (bf16[256,384]{1,0:T(8,128)(2,1)S(1)}, bf16[256,384]{1,0:T(8,128)(2,1)S(1)}) custom-call(bf16[1024,384]{1,0:T(8,128)(2,1)S(1)} %bitcast.8, f32[8,768]{1,0:T(8,128)S(1)} %get-tuple-element.26.small_ref, s32[1,1024]{1,0:T(1,128)S(1)} %get-tuple-element.28.place_ref), custom_call_target="tpu_custom_call" | custom-call | tf_op jit(solution)/shard_map/unpack_first/pallas_call | solution.py:454
  30.4 1.0 %collective-permute-start = (bf16[256,384]{1,0:T(8,128)(2,1)S(1)}, bf16[256,384]{1,0:T(8,128)(2,1)S(1)}, u32[]{:S(2)}, u32[]{:S(2)}) collective-permute-start(bf16[256,384]{1,0:T(8,128)(2,1)S(1)} %get-tuple-element.29.first_ref), channel_id=1, source_target_pairs={{0,1},{1,2},{2,3},{3,4},{4,5},{5,6},{6,7},{7,8},{8,9},{9,10},{10,1... | collective-permute-start | bytes 589832 | tf_op jit(solution)/shard_map/ppermute | solution.py:46
  31.4 0.0 copy-done.1
  31.4 2.4 %local_conv.1 = (f32[256,384]{1,0:T(8,128)S(1)}, f32[256,384]{1,0:T(8,128)S(1)}) custom-call(f32[8,128]{1,0:T(8,128)S(1)} %get-tuple-element.25.keep_ref, f32[8,768]{1,0:T(8,128)S(1)} %get-tuple-element.26.small_ref, bf16[256,384]{1,0:T(8,128)(2,1)S(1)} %get-tuple-element.29.first_ref, bf16[256,384]{1,0:T(8,128)(2,1)S(1)} %get-tuple-element.31.second_ref, ...), custom_call_target="tpu_custom_call" | custom-call | flops 2038431744 | tf_op jit(solution)/shard_map/local_conv/pallas_call | solution.py:454
  33.8 3.5 %collective-permute-done.1.prior_ref = bf16[256,384]{1,0:T(8,128)(2,1)S(1)} collective-permute-done((bf16[256,384]{1,0:T(8,128)(2,1)S(1)}, bf16[256,384]{1,0:T(8,128)(2,1)S(1)}, u32[]{:S(2)}, u32[]{:S(2)}) %collective-permute-start.1) | collective-permute-done | bytes 196640 | tf_op jit(solution)/shard_map/ppermute | solution.py:46
  37.4 0.0 copy-done
  37.4 0.1 collective-permute-start.3
  37.5 0.0 copy-start.3
  37.5 0.0 copy-start.2
  37.5 1.9 %collective-permute-done.prior_ref = bf16[256,384]{1,0:T(8,128)(2,1)S(1)} collective-permute-done((bf16[256,384]{1,0:T(8,128)(2,1)S(1)}, bf16[256,384]{1,0:T(8,128)(2,1)S(1)}, u32[]{:S(2)}, u32[]{:S(2)}) %collective-permute-start) | collective-permute-done | bytes 196640 | tf_op jit(solution)/shard_map/ppermute | solution.py:46
  39.5 0.2 collective-permute-start.2
  39.7 0.0 copy-done.3
  39.7 0.8 %local_time.1 = (f32[256,768]{1,0:T(8,128)S(1)}, f32[256,768]{1,0:T(8,128)S(1)}) custom-call(f32[8,128]{1,0:T(8,128)S(1)} %get-tuple-element.25.keep_ref, f32[8,768]{1,0:T(8,128)S(1)} %get-tuple-element.26.small_ref, bf16[256,384]{1,0:T(8,128)(2,1)S(1)} %first_residual.1.first_ref, bf16[256,384]{1,0:T(8,128)(2,1)S(1)} %second_residual.1.second_ref, ...), custom_call_target="tpu_custom_call" | custom-call | flops 271790912 | tf_op jit(solution)/shard_map/local_time/pallas_call | solution.py:454
  40.5 0.0 copy-done.2
  40.5 4.5 %early_up.1.early_hbm = bf16[4,32,6144]{2,1,0:T(8,128)(2,1)} custom-call(s32[1]{0:T(128)S(4)} %get-tuple-element.24.solo_ref, f32[8,768]{1,0:T(8,128)S(1)} %get-tuple-element.26.small_ref, f32[256,768]{1,0:T(8,128)S(1)} %get-tuple-element.38.sum0_ref.sum_ref, f32[256,768]{1,0:T(8,128)S(1)} %get-tuple-element.40.sum_ref.sum1_ref, ...), custom_call_target="tpu_custom_call" | custom-call | flops 1358954496 | tf_op jit(solution)/shard_map/early_up/pallas_call | solution.py:454
  45.0 0.3 collective-permute-done.3.prior_ref
  45.3 2.1 %collective-permute-done.2.before_ref = bf16[256,384]{1,0:T(8,128)(2,1)S(1)} collective-permute-done((bf16[256,384]{1,0:T(8,128)(2,1)S(1)}, bf16[256,384]{1,0:T(8,128)(2,1)S(1)}, u32[]{:S(2)}, u32[]{:S(2)}) %collective-permute-start.2) | collective-permute-done | bytes 196640 | tf_op jit(solution)/shard_map/ppermute | solution.py:46
  (14 shorter events, 0.1 us)
Async XLA Ops:
  0.0 10.0 %copy-start.7 = (f32[384]{0:T(512)S(1)}, f32[384]{0:T(512)}, u32[]{:S(2)}) copy-start(f32[384]{0:T(512)} %param.14) | copy-start | bytes 4612
  0.0 10.0 %copy-start.8 = (f32[384]{0:T(512)S(1)}, f32[384]{0:T(512)}, u32[]{:S(2)}) copy-start(f32[384]{0:T(512)} %param.15) | copy-start | bytes 4612
  0.0 10.0 %copy-start.9 = (f32[384]{0:T(512)S(1)}, f32[384]{0:T(512)}, u32[]{:S(2)}) copy-start(f32[384]{0:T(512)} %param.17) | copy-start | bytes 4612
  0.0 10.0 %copy-start.6 = (f32[768]{0:T(1024)S(1)}, f32[768]{0:T(1024)}, u32[]{:S(2)}) copy-start(f32[768]{0:T(1024)} %param.19) | copy-start | bytes 9220
  0.0 10.1 %copy-start.4 = (f32[192]{0:T(256)S(1)}, f32[192]{0:T(256)}, u32[]{:S(2)}) copy-start(f32[192]{0:T(256)} %param.21) | copy-start | bytes 2308
  0.0 10.1 %copy-start.5 = (s32[8]{0:T(128)S(1)}, s32[8]{0:T(128)}, u32[]{:S(2)}) copy-start(s32[8]{0:T(128)} %counts_ref.1) | copy-start | bytes 100
  2.6 26.1 %all-to-all-start = ((bf16[16,64,384]{2,1,0:T(8,128)(2,1)}), bf16[16,64,384]{2,1,0:T(8,128)(2,1)S(1)}, u32[]{:S(2)}, u32[]{:S(2)}) async-start(bf16[16,64,384]{2,1,0:T(8,128)(2,1)} %bitcast.5), calls=%async_computation | async-start | bytes 1572864 | tf_op jit(solution)/shard_map/all_to_all | solution.py:409
  28.7 2.7 %copy-start.1 = (bf16[3456,384]{1,0:T(8,128)(2,1)S(1)}, bf16[3456,384]{1,0:T(8,128)(2,1)}, u32[]{:S(2)}) copy-start(bf16[3456,384]{1,0:T(8,128)(2,1)} %get-tuple-element.32.behind_ref) | copy-start | bytes 7962628
  29.5 7.8 %collective-permute-start.1 = (bf16[256,384]{1,0:T(8,128)(2,1)S(1)}, bf16[256,384]{1,0:T(8,128)(2,1)S(1)}, u32[]{:S(2)}, u32[]{:S(2)}) collective-permute-start(bf16[256,384]{1,0:T(8,128)(2,1)S(1)} %get-tuple-element.31.second_ref), channel_id=1, source_target_pairs={{0,1},{1,2},{2,3},{3,4},{4,5},{5,6},{6,7},{7,8},{8,9},{9,10},{10,1... | collective-permute-start | bytes 589832 | tf_op jit(solution)/shard_map/ppermute | solution.py:46
  30.4 9.1 %collective-permute-start = (bf16[256,384]{1,0:T(8,128)(2,1)S(1)}, bf16[256,384]{1,0:T(8,128)(2,1)S(1)}, u32[]{:S(2)}, u32[]{:S(2)}) collective-permute-start(bf16[256,384]{1,0:T(8,128)(2,1)S(1)} %get-tuple-element.29.first_ref), channel_id=1, source_target_pairs={{0,1},{1,2},{2,3},{3,4},{4,5},{5,6},{6,7},{7,8},{8,9},{9,10},{10,1... | collective-permute-start | bytes 589832 | tf_op jit(solution)/shard_map/ppermute | solution.py:46
  31.4 6.0 %copy-start = (bf16[3456,384]{1,0:T(8,128)(2,1)S(1)}, bf16[3456,384]{1,0:T(8,128)(2,1)}, u32[]{:S(2)}) copy-start(bf16[3456,384]{1,0:T(8,128)(2,1)} %get-tuple-element.30.far_ref) | copy-start | bytes 7962628
  37.4 7.8 %collective-permute-start.3 = (bf16[256,384]{1,0:T(8,128)(2,1)S(1)}, bf16[256,384]{1,0:T(8,128)(2,1)S(1)}, u32[]{:S(2)}, u32[]{:S(2)}) collective-permute-start(bf16[256,384]{1,0:T(8,128)(2,1)S(1)} %second_residual.1.second_ref), channel_id=1, source_target_pairs={{0,1},{1,2},{2,3},{3,4},{4,5},{5,6},{6,7},{7,8},{8,9},{9,10},{10,1... | collective-permute-start | bytes 589832 | tf_op jit(solution)/shard_map/ppermute | solution.py:46
  37.5 2.3 %copy-start.3 = (bf16[3,384,768]{2,1,0:T(8,128)(2,1)S(1)}, bf16[3,384,768]{2,1,0:T(8,128)(2,1)}, u32[]{:S(2)}) copy-start(bf16[3,384,768]{2,1,0:T(8,128)(2,1)} %time_ref.5) | copy-start | bytes 5308420
  37.5 3.0 %copy-start.2 = (bf16[2,3,768,192]{3,2,1,0:T(8,128)(2,1)S(1)}, bf16[2,3,768,192]{3,2,1,0:T(8,128)(2,1)}, u32[]{:S(2)}) copy-start(bf16[2,3,768,192]{3,2,1,0:T(8,128)(2,1)} %get-tuple-element.39.folded_ref) | copy-start | bytes 5308420
  39.5 7.8 %collective-permute-start.2 = (bf16[256,384]{1,0:T(8,128)(2,1)S(1)}, bf16[256,384]{1,0:T(8,128)(2,1)S(1)}, u32[]{:S(2)}, u32[]{:S(2)}) collective-permute-start(bf16[256,384]{1,0:T(8,128)(2,1)S(1)} %first_residual.1.first_ref), channel_id=1, source_target_pairs={{0,1},{1,2},{2,3},{3,4},{4,5},{5,6},{6,7},{7,8},{8,9},{9,10},{10,1... | collective-permute-start | bytes 589832 | tf_op jit(solution)/shard_map/ppermute | solution.py:46
